TPU v7x, 32 devices: a whole 2x2x4 slice. The times are simulated.
32 devices in a mesh: dp: 16 (over z, y, x), shard: 2 (over core).
Axes of the slice: x: 2, y: 2, z: 4, core: 2. Of those that a mesh axis runs over, the one named last changes fastest.
Arguments:
- tokens: bfloat16 [16384, 1024], P(('dp', 'shard')), may hold values from -6 to 6
- cotangent: bfloat16 [16384, 1024], P(('dp', 'shard')), may hold values from -6 to 6
- lengths: int32 [32], P(('dp', 'shard')), may hold values from 1 to 512, as said below
- w_in: float32 [1024, 10240], P('shard'), may hold values from -0.1875 to 0.1875
- w_out: float32 [5120, 1024], P('shard')
- gains: float32 [2304], P('shard'), may hold values from 0.5 to 1.5
- first_in: float32 [1024, 10240], P('shard'), may hold values from -48 to 48
- first_out: float32 [5120, 1024], P('shard'), may hold values from -48 to 48
- gain_first: float32 [2304], P('shard'), may hold values from -96 to 96
- second_in: float32 [1024, 10240], P('shard'), may hold values from 212.992 to 868.352
- second_out: float32 [5120, 1024], P('shard'), may hold values from 212.992 to 868.352
- gain_second: float32 [2304], P('shard'), may hold values from 851.968 to 3440.64
Outputs:
- layer_output: bfloat16 [16384, 1024], P(('dp', 'shard'))
- layer_input_gradient: bfloat16 [16384, 1024], P(('dp', 'shard'))
- new_w_in: float32 [1024, 10240], P('shard')
- new_w_out: float32 [5120, 1024], P('shard')
- new_gains: float32 [2304], P('shard')
- new_first_in: float32 [1024, 10240], P('shard')
- new_first_out: float32 [5120, 1024], P('shard')
- new_gain_first: float32 [2304], P('shard')
- new_second_in: float32 [1024, 10240], P('shard')
- new_second_out: float32 [5120, 1024], P('shard')
- new_gain_second: float32 [2304], P('shard')
- valid_rms: float32 [2], replicated
Inputs may be any that keep to these rules, and one draw needn't show every extreme that they name: `lengths`: valid tokens of each slot, counted from its first row; in every draw one slot holds exactly 512.
All inputs are finite; a program needn't handle non-finite values.
Results may differ from a plain program's by a relative error of at most 0.013.
The roundings to bfloat16 on the way count: a program that leaves them out, or rounds other values in their place, can miss the bound.
Values may be sent and summed in bfloat16 or wider, within the bound.
No kernel may reach another device: no remote copies, remote signals or barrier semaphores. Data moves between devices by JAX's collectives and lax.ppermute only.
A program may use at most 448 MiB of HBM per device.

v0:
```python
import functools
import math

import jax
import jax.numpy as jnp
import numpy as np
from jax import lax
from jax.experimental import pallas as pl
from jax.experimental.pallas import tpu as pltpu
from jax.sharding import PartitionSpec as P

MODEL_WIDTH = 1024
FF = 3072
QUERY_HEADS = 16
KEY_VALUE_HEADS = 8
HEAD_SIZE = 128
SLOT_ROWS = 512
STEP = 7
QKVC = 4096
GN = 2304


EPSILON = 1e-06
BETA_ONE = 0.9
BETA_TWO = 0.95
ADAM_EPSILON = 1e-08
MATRIX_RATE = 0.05
GAIN_RATE = 0.3
MATRIX_DECAY = 0.1
NEG_LARGE = -1e30


def rms_scale(values, gain):
    return values * lax.rsqrt(jnp.mean(values * values, axis=-1, keepdims=True) + EPSILON) * gain


def rope_tables(length, size):
    positions = jnp.arange(length, dtype=jnp.float32)
    half_index = jnp.arange(size // 2, dtype=jnp.float32)
    frequency = jnp.exp(half_index * (-2.0 * math.log(1000000.0) / size))
    angles = positions[:, None] * frequency[None, :]
    angles = jnp.concatenate([angles, angles], axis=1)
    return (jnp.cos(angles), jnp.sin(angles))


def rotate(values, cosine, sine):
    half_size = values.shape[-1] // 2
    turned = jnp.concatenate([-values[..., half_size:], values[..., :half_size]], axis=-1)
    return values * cosine[:, None, :] + turned * sine[:, None, :]


def prepare(unnormed_rows, gain_q, gain_k, cosine, sine):
    leading_rows = unnormed_rows.shape[:-1]
    queries = unnormed_rows[..., : QUERY_HEADS * HEAD_SIZE].reshape(
        leading_rows + (QUERY_HEADS, HEAD_SIZE)
    )
    key_head_rows = unnormed_rows[
        ..., QUERY_HEADS * HEAD_SIZE : (QUERY_HEADS + KEY_VALUE_HEADS) * HEAD_SIZE
    ].reshape(leading_rows + (KEY_VALUE_HEADS, HEAD_SIZE))
    value_head_rows = unnormed_rows[..., (QUERY_HEADS + KEY_VALUE_HEADS) * HEAD_SIZE :].reshape(
        leading_rows + (KEY_VALUE_HEADS, HEAD_SIZE)
    )
    queries = rotate(rms_scale(queries, gain_q), cosine, sine)
    key_head_rows = rotate(rms_scale(key_head_rows, gain_k), cosine, sine)
    return (queries, key_head_rows, value_head_rows)


def gated_unit(mixed):
    return jax.nn.silu(mixed[..., :FF]) * mixed[..., FF:]


def adamw_update(weight, first, second, gradient, rate, decay):
    first = BETA_ONE * first + (1.0 - BETA_ONE) * gradient
    second = BETA_TWO * second + (1.0 - BETA_TWO) * gradient * gradient
    corr_one = 1.0 - BETA_ONE**STEP
    corr_two = 1.0 - BETA_TWO**STEP
    update = first / corr_one / (jnp.sqrt(second / corr_two) + ADAM_EPSILON) + decay * weight
    return (weight - rate * update, first, second)


def outer_sum(left, right):
    return lax.dot_general(
        left, right, (((0,), (0,)), ((), ())), preferred_element_type=jnp.float32
    )


def back_product(gradient, weight):
    return lax.dot_general(
        gradient, weight, (((1,), (1,)), ((), ())), preferred_element_type=jnp.float32
    )


def key_mask(row_count, key_reach, length):
    query_pos = jnp.arange(row_count, dtype=jnp.int32)
    key_pos = jnp.arange(key_reach, dtype=jnp.int32)
    return (key_pos[None, :] <= query_pos[:, None]) & (key_pos[None, :] < length)


def slot_attention(query_low, key_low, value_low, length):
    block_rows = min(512, SLOT_ROWS)
    score_scale = HEAD_SIZE ** (-0.5)
    scores = (
        jnp.einsum("hgqd,hkd->hgqk", query_low, key_low, preferred_element_type=jnp.float32)
        * score_scale
    )
    scores = jnp.where(key_mask(block_rows, block_rows, length), scores, NEG_LARGE)
    row_peak = jnp.max(scores, axis=-1, keepdims=True)
    exp_values = jnp.exp(scores - row_peak)
    exp_total = jnp.sum(exp_values, axis=-1, keepdims=True)
    soft_weights = (exp_values / exp_total).astype(jnp.bfloat16)
    outputs = [
        jnp.einsum(
            "hgqk,hkd->hgqd", soft_weights, value_low, preferred_element_type=jnp.float32
        ).astype(jnp.bfloat16)
    ]
    totals = [row_peak + jnp.log(exp_total)]
    return (jnp.concatenate(outputs, axis=2), jnp.concatenate(totals, axis=2))


def slot_attention_back(query_low, key_low, value_low, totals, heads_gradient, length):
    block_rows = min(512, SLOT_ROWS)
    score_scale = HEAD_SIZE ** (-0.5)
    grad_keys = jnp.zeros(key_low.shape, jnp.float32)
    value_gradients = jnp.zeros(value_low.shape, jnp.float32)
    scores = (
        jnp.einsum("hgqd,hkd->hgqk", query_low, key_low, preferred_element_type=jnp.float32)
        * score_scale
    )
    allowed = key_mask(block_rows, block_rows, length)
    soft_weights = jnp.where(allowed, jnp.exp(scores - totals[:, :, 0:block_rows]), 0.0)
    back_soft = jnp.einsum(
        "hgqd,hkd->hgqk", heads_gradient, value_low, preferred_element_type=jnp.float32
    )
    inner_sums = jnp.sum(soft_weights * back_soft, axis=-1, keepdims=True)
    back_scores = (soft_weights * (back_soft - inner_sums)).astype(jnp.bfloat16)
    query_parts = [
        jnp.einsum("hgqk,hkd->hgqd", back_scores, key_low, preferred_element_type=jnp.float32)
        * score_scale
    ]
    grad_keys = grad_keys.at[:, :block_rows].add(
        jnp.einsum("hgqk,hgqd->hkd", back_scores, query_low, preferred_element_type=jnp.float32)
        * score_scale
    )
    value_gradients = value_gradients.at[:, :block_rows].add(
        jnp.einsum(
            "hgqk,hgqd->hkd",
            soft_weights.astype(jnp.bfloat16),
            heads_gradient,
            preferred_element_type=jnp.float32,
        )
    )
    return (jnp.concatenate(query_parts, axis=2), grad_keys, value_gradients)


def shards(
    tokens,
    cotangent,
    lengths,
    w_in,
    w_out,
    gains,
    first_in,
    first_out,
    gain_first,
    second_in,
    second_out,
    gain_second,
):
    slot_batch = lengths.shape[0]
    row_total = tokens.shape[0]
    query_group_width = QUERY_HEADS // KEY_VALUE_HEADS
    gathered_in, gathered_out, gathered_gains = (
        lax.all_gather(w_in.astype(jnp.bfloat16), "shard", axis=0, tiled=True),
        lax.all_gather(w_out.astype(jnp.bfloat16), "shard", axis=0, tiled=True),
        lax.all_gather(gains.astype(jnp.bfloat16), "shard", axis=0, tiled=True),
    )
    gain_all = gathered_gains.astype(jnp.float32)
    gain_in = gain_all[:MODEL_WIDTH]
    gain_post = gain_all[MODEL_WIDTH : 2 * MODEL_WIDTH]
    gain_query = gain_all[2 * MODEL_WIDTH : 2 * MODEL_WIDTH + HEAD_SIZE]
    gain_key = gain_all[2 * MODEL_WIDTH + HEAD_SIZE :]
    proj_qkv = gathered_in[:, :QKVC]
    proj_mix = gathered_in[:, QKVC:]
    proj_attn = gathered_out[: QUERY_HEADS * HEAD_SIZE]
    proj_down = gathered_out[QUERY_HEADS * HEAD_SIZE :]
    cosine, sine = rope_tables(SLOT_ROWS, HEAD_SIZE)
    layer_inputs = tokens.astype(jnp.float32)
    normed, pull_in = jax.vjp(rms_scale, layer_inputs, gain_in)
    normed_low = normed.astype(jnp.bfloat16)
    unnormed_rows = jnp.dot(normed_low, proj_qkv, preferred_element_type=jnp.float32).reshape(
        slot_batch, SLOT_ROWS, QKVC
    )

    def prep_local(raw_part, gain_q, gain_k):
        return prepare(raw_part, gain_q, gain_k, cosine, sine)

    (queries, key_head_rows, value_head_rows), pull_prep = jax.vjp(
        prep_local, unnormed_rows, gain_query, gain_key
    )
    query_low = (
        queries.astype(jnp.bfloat16)
        .reshape(slot_batch, SLOT_ROWS, KEY_VALUE_HEADS, query_group_width, HEAD_SIZE)
        .transpose(0, 2, 3, 1, 4)
    )
    key_low = key_head_rows.astype(jnp.bfloat16).transpose(0, 2, 1, 3)
    value_low = value_head_rows.astype(jnp.bfloat16).transpose(0, 2, 1, 3)
    attended, totals = lax.map(
        lambda slot_item: slot_attention(slot_item[0], slot_item[1], slot_item[2], slot_item[3]),
        (query_low, key_low, value_low, lengths),
    )
    attended_rows = attended.transpose(0, 3, 1, 2, 4).reshape(row_total, QUERY_HEADS * HEAD_SIZE)
    middle = layer_inputs + jnp.dot(attended_rows, proj_attn, preferred_element_type=jnp.float32)
    normed_post, pull_post = jax.vjp(rms_scale, middle, gain_post)
    post_low = normed_post.astype(jnp.bfloat16)
    mixed = jnp.dot(post_low, proj_mix, preferred_element_type=jnp.float32)
    hidden, pull_gate = jax.vjp(gated_unit, mixed)
    hidden_low = hidden.astype(jnp.bfloat16)
    layer_output = (
        middle + jnp.dot(hidden_low, proj_down, preferred_element_type=jnp.float32)
    ).astype(jnp.bfloat16)
    positions = jnp.arange(SLOT_ROWS, dtype=jnp.int32)
    valid_row_count = (
        (positions[None, :] < lengths[:, None]).astype(jnp.float32).reshape(row_total, 1)
    )
    back_out = cotangent.astype(jnp.float32) * valid_row_count
    back_out_low = back_out.astype(jnp.bfloat16)
    grad_down = outer_sum(hidden_low, back_out_low)
    back_hidden = back_product(back_out_low, proj_down)
    (back_mixed,) = pull_gate(back_hidden)
    mixed_low = back_mixed.astype(jnp.bfloat16)
    grad_mix = outer_sum(post_low, mixed_low)
    back_post = back_product(mixed_low, proj_mix)
    back_middle, grad_gain_post = pull_post(back_post)
    back_middle = back_middle + back_out
    middle_low = back_middle.astype(jnp.bfloat16)
    grad_attn = outer_sum(attended_rows, middle_low)
    attended_gradient = back_product(middle_low, proj_attn).astype(jnp.bfloat16)
    heads_gradient = attended_gradient.reshape(
        slot_batch, SLOT_ROWS, KEY_VALUE_HEADS, query_group_width, HEAD_SIZE
    ).transpose(0, 2, 3, 1, 4)
    grad_query, grad_key, grad_value = lax.map(
        lambda slot_item: slot_attention_back(
            slot_item[0], slot_item[1], slot_item[2], slot_item[3], slot_item[4], slot_item[5]
        ),
        (query_low, key_low, value_low, totals, heads_gradient, lengths),
    )
    grad_query = grad_query.transpose(0, 3, 1, 2, 4).reshape(
        slot_batch, SLOT_ROWS, QUERY_HEADS, HEAD_SIZE
    )
    grad_key = grad_key.transpose(0, 2, 1, 3)
    grad_value = grad_value.transpose(0, 2, 1, 3)
    back_raw, grad_gain_query, grad_gain_key = pull_prep((grad_query, grad_key, grad_value))
    raw_low = back_raw.reshape(row_total, QKVC).astype(jnp.bfloat16)
    grad_qkv = outer_sum(normed_low, raw_low)
    back_normed = back_product(raw_low, proj_qkv)
    back_inputs, grad_gain_in = pull_in(back_normed)
    layer_input_gradient = (back_middle + back_inputs).astype(jnp.bfloat16)
    output_values = layer_output.astype(jnp.float32)
    value_gradients = layer_input_gradient.astype(jnp.float32)
    sum_out, sum_grad, sum_count = lax.psum(
        (
            jnp.sum(valid_row_count * output_values * output_values),
            jnp.sum(valid_row_count * value_gradients * value_gradients),
            jnp.sum(valid_row_count),
        ),
        ("dp", "shard"),
    )
    valid_rms = jnp.sqrt(jnp.stack([sum_out, sum_grad]) / (sum_count * MODEL_WIDTH))
    owners = lax.axis_size("shard")
    grad_in = jnp.concatenate([grad_qkv, grad_mix], axis=1)
    grad_out = jnp.concatenate([grad_attn, grad_down], axis=0)
    grad_gain = jnp.concatenate(
        [grad_gain_in, grad_gain_post, grad_gain_query, grad_gain_key]
    ).reshape(owners, GN // owners)
    part_in, part_out, part_gain = (
        lax.psum_scatter(grad_in, "dp", scatter_dimension=1, tiled=True),
        lax.psum_scatter(grad_out, "dp", scatter_dimension=1, tiled=True),
        lax.psum_scatter(grad_gain, "dp", scatter_dimension=1, tiled=True),
    )
    owned_in, owned_out, owned_gain = (
        lax.psum_scatter(part_in, "shard", scatter_dimension=0, tiled=True),
        lax.psum_scatter(part_out, "shard", scatter_dimension=0, tiled=True),
        lax.psum_scatter(part_gain, "shard", scatter_dimension=0, tiled=True),
    )
    summed_in, summed_out, summed_gain = (
        lax.all_gather(owned_in, "dp", axis=1, tiled=True),
        lax.all_gather(owned_out, "dp", axis=1, tiled=True),
        lax.all_gather(owned_gain, "dp", axis=1, tiled=True),
    )
    summed_gain = summed_gain.reshape(-1)
    new_w_in, new_first_in, new_second_in = adamw_update(
        w_in, first_in, second_in, summed_in, MATRIX_RATE, MATRIX_DECAY
    )
    new_w_out, new_first_out, new_second_out = adamw_update(
        w_out, first_out, second_out, summed_out, MATRIX_RATE, MATRIX_DECAY
    )
    new_gains, new_gain_first, new_gain_second = adamw_update(
        gains, gain_first, gain_second, summed_gain, GAIN_RATE, 0.0
    )
    return (
        layer_output,
        layer_input_gradient,
        new_w_in,
        new_w_out,
        new_gains,
        new_first_in,
        new_first_out,
        new_gain_first,
        new_second_in,
        new_second_out,
        new_gain_second,
        valid_rms,
    )


def low(values):
    return values.astype(jnp.bfloat16)


def wide(values):
    return values.astype(jnp.float32)


def mul(left, right):
    return jnp.dot(left, right, preferred_element_type=jnp.float32)


def mul_bt(left, right):
    return lax.dot_general(
        left, right, (((1,), (1,)), ((), ())), preferred_element_type=jnp.float32
    )


def mul_at(left, right):
    return lax.dot_general(
        left, right, (((0,), (0,)), ((), ())), preferred_element_type=jnp.float32
    )


def whole(shape):
    return pl.BlockSpec(shape, lambda *_: (0,) * len(shape))


def resident(shape, index=None):
    index = index or (0,) * len(shape)
    return pl.BlockSpec(shape, lambda *_: index, pipeline_mode=pl.Buffered(1))


def shape_of(shape, kind):
    return jax.ShapeDtypeStruct(shape, kind)


GAIN_IN = slice(0, MODEL_WIDTH)
GAIN_POST = slice(MODEL_WIDTH, 2 * MODEL_WIDTH)
GAIN_Q = slice(2 * MODEL_WIDTH, 2 * MODEL_WIDTH + HEAD_SIZE)
GAIN_K = slice(2 * MODEL_WIDTH + HEAD_SIZE, GN)
BF = jnp.bfloat16
F32 = jnp.float32
VMEM_BYTES = 64 * 1024 * 1024


def params(axes=1, limit=VMEM_BYTES):
    return pltpu.CompilerParams(
        dimension_semantics=("arbitrary",) * axes, vmem_limit_bytes=limit
    )


def split_columns(values, core):
    half = values.shape[1] // 2
    first, second = values[:, :half], values[:, half:]
    mine = core == 0
    return jnp.where(mine, first, second), jnp.where(mine, second, first)


def join_columns(own, other, core):
    mine = core == 0
    return jnp.concatenate(
        [jnp.where(mine, own, other), jnp.where(mine, other, own)], axis=1
    )


def cast_qkv_kernel(q_ref, k_ref, v_ref, out_ref):
    for at in range(out_ref.shape[0]):
        out_ref[at, :, :256] = low(q_ref[:, at * 256 : at * 256 + 256])
        out_ref[at, :, 256:384] = low(k_ref[:, at * 128 : at * 128 + 128])
        out_ref[at, :, 384:] = low(v_ref[:, at * 128 : at * 128 + 128])


def cast_qkv(w_in):
    rows = w_in.shape[0]
    width = 256
    return pl.pallas_call(
        cast_qkv_kernel,
        grid=(KEY_VALUE_HEADS * 128 // width,),
        in_specs=[
            pl.BlockSpec((rows, 2 * width), lambda g: (0, g)),
            pl.BlockSpec((rows, width), lambda g: (0, 2048 // width + g)),
            pl.BlockSpec((rows, width), lambda g: (0, 3072 // width + g)),
        ],
        out_specs=pl.BlockSpec((width // 128, rows, 512), lambda g: (g, 0, 0)),
        out_shape=shape_of((KEY_VALUE_HEADS, rows, 512), BF),
        compiler_params=params(),
        name="cast_qkv",
    )(w_in, w_in, w_in)


def cast_rows_kernel(in_ref, out_ref):
    out_ref[...] = low(in_ref[...])


def cast_rows(values, block):
    rows, columns = values.shape
    spec = pl.BlockSpec((block, columns), lambda i: (i, 0))
    return pl.pallas_call(
        cast_rows_kernel,
        grid=(rows // block,),
        in_specs=[spec],
        out_specs=spec,
        out_shape=shape_of(values.shape, BF),
        compiler_params=params(),
        name="cast_out",
    )(values)


def cast_mix_kernel(gate_ref, up_ref, *out_refs):
    half = gate_ref.shape[0] // 2
    for at, out_ref in enumerate(out_refs):
        rows = slice(at * half, at * half + half)
        out_ref[0, :, :FFB] = low(gate_ref[rows, :])
        out_ref[0, :, FFB:] = low(up_ref[rows, :])


FFB = 1024
FF_STEPS = FF // FFB


def cast_mix(w_in):
    rows = w_in.shape[0]
    return pl.pallas_call(
        cast_mix_kernel,
        grid=(FF_STEPS,),
        in_specs=[
            pl.BlockSpec((rows, FFB), lambda j: (0, QKVC // FFB + j)),
            pl.BlockSpec((rows, FFB), lambda j: (0, (QKVC + FF) // FFB + j)),
        ],
        out_specs=[pl.BlockSpec((1, rows // 2, 2 * FFB), lambda j: (j, 0, 0))] * 2,
        out_shape=[shape_of((FF_STEPS, rows // 2, 2 * FFB), BF)] * 2,
        compiler_params=params(),
        name="cast_mix",
    )(w_in, w_in)


def turn(values):
    return pltpu.roll(values, HEAD_SIZE // 2, 1)


def head_norm(raw):
    scale = lax.rsqrt(jnp.mean(raw * raw, axis=-1, keepdims=True) + EPSILON)
    return raw * scale, scale


def block_mask(first_row, rows, keys, length):
    row = first_row + lax.broadcasted_iota(jnp.int32, (2 * rows, keys), 0) % rows
    key = lax.broadcasted_iota(jnp.int32, (2 * rows, keys), 1)
    return (key <= row) & (key < length)


def both_heads(values):
    return jnp.concatenate([values[:, :128], values[:, 128:]], axis=0)


QB = 128


def forward_kernel(
    meta_ref,
    x_ref,
    gain_ref,
    cos_ref,
    sin_ref,
    own_ref,
    other_ref,
    o_ref,
    qkv_ref,
    u_ref,
    lse_ref,
    a_own_ref,
    a_other_ref,
):
    core, length = meta_ref[0], meta_ref[1]

    @pl.when(pl.program_id(0) == 0)
    def _():
        x = wide(x_ref[...])
        scale = lax.rsqrt(jnp.mean(x * x, axis=-1, keepdims=True) + EPSILON)
        own, other = split_columns(low(x * scale * gain_ref[:, GAIN_IN]), core)
        a_own_ref[...] = own
        a_other_ref[...] = other

    u = mul(a_own_ref[...], own_ref[0]) + mul(a_other_ref[...], other_ref[0])
    u_ref[0] = u[:, :384]
    cosine, sine = cos_ref[...], sin_ref[...]
    gain_q, gain_k = gain_ref[:, GAIN_Q], gain_ref[:, GAIN_K]
    for part in range(3):
        normed, _ = head_norm(u[:, part * 128 : part * 128 + 128])
        normed = normed * (gain_k if part == 2 else gain_q)
        qkv_ref[0, :, part * 128 : part * 128 + 128] = low(
            normed * cosine + turn(normed) * sine
        )
    qkv_ref[0, :, 384:] = low(u[:, 384:])
    score_scale = HEAD_SIZE ** (-0.5)
    for first in range(0, SLOT_ROWS, QB):
        keys = first + QB
        rows = slice(first, first + QB)
        k = qkv_ref[0, :keys, 256:384]
        v = qkv_ref[0, :keys, 384:]
        scores = mul_bt(both_heads(qkv_ref[0, rows, :256]), k) * score_scale
        scores = jnp.where(block_mask(first, QB, keys, length), scores, NEG_LARGE)
        peak = jnp.max(scores, axis=-1, keepdims=True)
        powers = jnp.exp(scores - peak)
        total = jnp.sum(powers, axis=-1, keepdims=True)
        o = low(mul(low(powers * (1.0 / total)), v))
        level = peak + jnp.log(total)
        for head in range(2):
            half = slice(head * QB, head * QB + QB)
            columns = slice(head * 128, head * 128 + 128)
            o_ref[rows, columns] = o[half]
            lse_ref[0, rows, columns] = jnp.broadcast_to(level[half], (QB, 128))


def forward(meta, tokens, gains, cosine, sine, own, other):
    rows = SLOT_ROWS
    half = MODEL_WIDTH // 2
    return pl.pallas_call(
        forward_kernel,
        grid_spec=pltpu.PrefetchScalarGridSpec(
            num_scalar_prefetch=1,
            grid=(KEY_VALUE_HEADS,),
            in_specs=[
                resident((rows, MODEL_WIDTH)),
                resident((1, GN)),
                resident((rows, HEAD_SIZE)),
                resident((rows, HEAD_SIZE)),
                pl.BlockSpec((1, half, 512), lambda g, _: (g, 0, 0)),
                pl.BlockSpec((1, half, 512), lambda g, _: (g, 0, 0)),
            ],
            out_specs=[
                pl.BlockSpec((rows, 256), lambda g, _: (0, g)),
                pl.BlockSpec((1, rows, 512), lambda g, _: (g, 0, 0)),
                pl.BlockSpec((1, rows, 384), lambda g, _: (g, 0, 0)),
                pl.BlockSpec((1, rows, 256), lambda g, _: (g, 0, 0)),
                whole((rows, half)),
                whole((rows, half)),
            ],
        ),
        out_shape=[
            shape_of((rows, QUERY_HEADS * HEAD_SIZE), BF),
            shape_of((KEY_VALUE_HEADS, rows, 512), BF),
            shape_of((KEY_VALUE_HEADS, rows, 384), F32),
            shape_of((KEY_VALUE_HEADS, rows, 256), F32),
            shape_of((rows, half), BF),
            shape_of((rows, half), BF),
        ],
        compiler_params=params(),
        name="forward",
    )(meta, tokens, gains, cosine, sine, own, other)


def unit_kernel(
    meta_ref,
    o_ref,
    x_ref,
    e_ref,
    gain_ref,
    wo_ref,
    wd_ref,
    own_top_ref,
    own_end_ref,
    other_top_ref,
    other_end_ref,
    y_ref,
    dgate_ref,
    dup_ref,
    b_own_ref,
    b_other_ref,
    left_ref,
    send_ref,
    dmid_ref,
    dlow_ref,
    small_ref,
    mid_s,
    y_s,
    db_own_s,
    db_other_s,
):
    core, length = meta_ref[0], meta_ref[1]
    step = pl.program_id(0)
    quarter = own_top_ref.shape[1]
    weights = [
        (b_own_ref, slice(0, quarter), db_own_s, own_top_ref),
        (b_own_ref, slice(quarter, None), db_own_s, own_end_ref),
        (b_other_ref, slice(0, quarter), db_other_s, other_top_ref),
        (b_other_ref, slice(quarter, None), db_other_s, other_end_ref),
    ]
    attended = QUERY_HEADS * HEAD_SIZE
    valid = lax.broadcasted_iota(jnp.int32, (SLOT_ROWS, 1), 0) < length

    @pl.when(step == 0)
    def _():
        middle = wide(x_ref[...]) + mul(o_ref[...], wo_ref[...])
        mid_s[...] = middle
        y_s[...] = middle
        scale = lax.rsqrt(jnp.mean(middle * middle, axis=-1, keepdims=True) + EPSILON)
        own, other = split_columns(low(middle * scale * gain_ref[:, GAIN_POST]), core)
        b_own_ref[...] = own
        b_other_ref[...] = other
        db_own_s[...] = jnp.zeros_like(db_own_s)
        db_other_s[...] = jnp.zeros_like(db_other_s)

        @pl.when(core == 0)
        def _():
            left_ref[:, :attended] = o_ref[...]

        @pl.when(core != 0)
        def _():
            send_ref[:, :attended] = o_ref[...]

    e = e_ref[...]
    for part in range(FFB // 512):
        gates = slice(part * 512, part * 512 + 512)
        ups = slice(FFB + part * 512, FFB + part * 512 + 512)
        gate = sum(mul(b_ref[:, rows], w_ref[0, :, gates]) for b_ref, rows, _, w_ref in weights)
        up = sum(mul(b_ref[:, rows], w_ref[0, :, ups]) for b_ref, rows, _, w_ref in weights)
        down = wd_ref[gates, :]
        dh = mul_bt(e, down)
        sigma = 1.0 / (1.0 + jnp.exp(-gate))
        silu = gate * sigma
        hidden = low(silu * up)
        dgate = low(dh * up * (sigma * (1.0 + gate * (1.0 - sigma))))
        dup = low(dh * silu)
        y_s[...] += mul(hidden, down)
        for _, rows, db_s, w_ref in weights:
            db_s[:, rows] += mul_bt(dgate, w_ref[0, :, gates]) + mul_bt(dup, w_ref[0, :, ups])
        dgate_ref[:, gates] = dgate
        dup_ref[:, gates] = dup

        place = pl.multiple_of(jnp.maximum(step * FFB + part * 512 - 512, 0), 512)
        first_rows = (step == 0) & (part == 0)

        @pl.when(first_rows & (core == 0))
        def _():
            left_ref[:, attended:] = hidden

        @pl.when(first_rows & (core != 0))
        def _():
            send_ref[:, attended : attended + 512] = hidden

        @pl.when(jnp.logical_not(first_rows) & (core == 0))
        def _():
            send_ref[:, pl.ds(place, 512)] = hidden

        @pl.when(jnp.logical_not(first_rows) & (core != 0))
        def _():
            left_ref[:, pl.ds(place, 512)] = hidden

    @pl.when(step == FF_STEPS - 1)
    def _():
        y = low(y_s[...])
        y_ref[...] = y
        y = wide(y)
        total = jnp.sum(jnp.where(valid, y * y, 0.0))
        db = join_columns(db_own_s[...], db_other_s[...], core)
        middle = mid_s[...]
        scale = lax.rsqrt(jnp.mean(middle * middle, axis=-1, keepdims=True) + EPSILON)
        normed = middle * scale
        dn = db * gain_ref[:, GAIN_POST]
        dmid = wide(e) + scale * (
            dn - normed * jnp.mean(dn * normed, axis=-1, keepdims=True)
        )
        dmid_ref[...] = dmid
        dlow = low(dmid)
        dlow_ref[...] = dlow
        send_ref[:, left_ref.shape[1] :] = dlow
        small_ref[0:1, :] = jnp.sum(db * normed, axis=0, keepdims=True)
        small_ref[1:8, :] = jnp.full((7, MODEL_WIDTH), total)


def unit(meta, o, tokens, e, gains, w_out, *mix):
    rows = SLOT_ROWS
    half = MODEL_WIDTH // 2
    attended = QUERY_HEADS * HEAD_SIZE
    owned = w_out.shape[0] // 2
    return pl.pallas_call(
        unit_kernel,
        grid_spec=pltpu.PrefetchScalarGridSpec(
            num_scalar_prefetch=1,
            grid=(FF_STEPS,),
            in_specs=[
                resident((rows, attended)),
                resident((rows, MODEL_WIDTH)),
                resident((rows, MODEL_WIDTH)),
                resident((1, GN)),
                resident((attended, MODEL_WIDTH)),
                pl.BlockSpec((FFB, MODEL_WIDTH), lambda j, _: (attended // FFB + j, 0)),
            ]
            + [pl.BlockSpec((1, half // 2, 2 * FFB), lambda j, _: (j, 0, 0))] * 4,
            out_specs=[
                whole((rows, MODEL_WIDTH)),
                pl.BlockSpec((rows, FFB), lambda j, _: (0, j)),
                pl.BlockSpec((rows, FFB), lambda j, _: (0, j)),
                whole((rows, half)),
                whole((rows, half)),
                whole((rows, owned)),
                whole((rows, owned + MODEL_WIDTH)),
                whole((rows, MODEL_WIDTH)),
                whole((rows, MODEL_WIDTH)),
                whole((8, MODEL_WIDTH)),
            ],
            scratch_shapes=[
                pltpu.VMEM((rows, MODEL_WIDTH), F32),
                pltpu.VMEM((rows, MODEL_WIDTH), F32),
                pltpu.VMEM((rows, half), F32),
                pltpu.VMEM((rows, half), F32),
            ],
        ),
        out_shape=[
            shape_of((rows, MODEL_WIDTH), BF),
            shape_of((rows, FF), BF),
            shape_of((rows, FF), BF),
            shape_of((rows, half), BF),
            shape_of((rows, half), BF),
            shape_of((rows, owned), BF),
            shape_of((rows, owned + MODEL_WIDTH), BF),
            shape_of((rows, MODEL_WIDTH), F32),
            shape_of((rows, MODEL_WIDTH), BF),
            shape_of((8, MODEL_WIDTH), F32),
        ],
        compiler_params=params(),
        name="unit",
    )(meta, o, tokens, e, gains, w_out, w_out, *mix)


def backward_kernel(
    meta_ref,
    dmid_ref,
    dlow_ref,
    x_ref,
    gain_ref,
    cos_ref,
    sin_ref,
    wo_ref,
    own_ref,
    other_ref,
    qkv_ref,
    u_ref,
    lse_ref,
    small_in_ref,
    dx_ref,
    duq_first_ref,
    duq_last_ref,
    duk_ref,
    duv_ref,
    small_ref,
    da_own_s,
    da_other_s,
    head_s,
    dk_s,
    dv_s,
):
    core, length = meta_ref[0], meta_ref[1]
    step = pl.program_id(0)

    @pl.when(step == 0)
    def _():
        for sums in (da_own_s, da_other_s, head_s):
            sums[...] = jnp.zeros_like(sums)

    cosine, sine = cos_ref[...], sin_ref[...]
    score_scale = HEAD_SIZE ** (-0.5)
    do = low(mul_bt(dlow_ref[...], wo_ref[...]))

    def through(grad, raw, gain, slot):
        back = grad * cosine - turn(grad) * sine
        normed, scale = head_norm(raw)
        head_s[slot : slot + 1, :] += jnp.sum(back * normed, axis=0, keepdims=True)
        dn = back * gain
        return low(scale * (dn - normed * jnp.mean(dn * normed, axis=-1, keepdims=True)))

    grad_rows = []
    for first in reversed(range(0, SLOT_ROWS, QB)):
        keys = first + QB
        rows = slice(first, first + QB)
        q = both_heads(qkv_ref[0, rows, :256])
        k = qkv_ref[0, :keys, 256:384]
        v = qkv_ref[0, :keys, 384:]
        dos = both_heads(do[rows, :])
        level = jnp.concatenate([lse_ref[0, rows, 0:1], lse_ref[0, rows, 128:129]], axis=0)
        soft = jnp.where(
            block_mask(first, QB, keys, length),
            jnp.exp(mul_bt(q, k) * score_scale - level),
            0.0,
        )
        dsoft = mul_bt(dos, v)
        inner = jnp.sum(soft * dsoft, axis=-1, keepdims=True)
        ds = low(soft * (dsoft - inner))
        grad_rows.insert(0, mul(ds, k))
        grad_k = mul_at(ds, q)
        grad_v = mul_at(low(soft), dos)
        if keys == SLOT_ROWS:
            dk_s[...] = grad_k
            dv_s[...] = grad_v
        else:
            dk_s[:keys, :] += grad_k
            dv_s[:keys, :] += grad_v
    parts = []
    for head in range(2):
        columns = slice(head * 128, head * 128 + 128)
        grad_q = jnp.concatenate([g[head * QB : head * QB + QB] for g in grad_rows], axis=0)
        parts.append(
            through(grad_q * score_scale, u_ref[0, :, columns], gain_ref[:, GAIN_Q], 0)
        )
    parts.append(
        through(dk_s[...] * score_scale, u_ref[0, :, 256:384], gain_ref[:, GAIN_K], 1)
    )
    parts.append(low(dv_s[...]))
    du = jnp.concatenate(parts, axis=1)
    duk_ref[...] = du[:, 256:384]
    duv_ref[...] = du[:, 384:]

    @pl.when(step < KEY_VALUE_HEADS // 2)
    def _():
        duq_first_ref[...] = du[:, :256]

    @pl.when(step >= KEY_VALUE_HEADS // 2)
    def _():
        duq_last_ref[...] = du[:, :256]

    da_own_s[...] += mul_bt(du, own_ref[0])
    da_other_s[...] += mul_bt(du, other_ref[0])

    @pl.when(step == KEY_VALUE_HEADS - 1)
    def _():
        da = join_columns(da_own_s[...], da_other_s[...], core)
        x = wide(x_ref[...])
        scale = lax.rsqrt(jnp.mean(x * x, axis=-1, keepdims=True) + EPSILON)
        normed = x * scale
        dn = da * gain_ref[:, GAIN_IN]
        dx = low(
            dmid_ref[...]
            + scale * (dn - normed * jnp.mean(dn * normed, axis=-1, keepdims=True))
        )
        dx_ref[...] = dx
        dx = wide(dx)
        valid = lax.broadcasted_iota(jnp.int32, (SLOT_ROWS, 1), 0) < length
        total = jnp.sum(jnp.where(valid, dx * dx, 0.0))
        small_ref[0:1, :] = jnp.sum(da * normed, axis=0, keepdims=True)
        small_ref[1:2, :] = small_in_ref[0:1, :]
        small_ref[2:8, :] = jnp.full((6, MODEL_WIDTH), total)
        small_ref[2:3, 0:128] = head_s[0:1, :]
        small_ref[2:3, 128:256] = head_s[1:2, :]
        small_ref[3:4, :] = small_in_ref[1:2, :]
        small_ref[4:5, :] = jnp.full((1, MODEL_WIDTH), 1.0) * length.astype(F32)


def backward(
    meta,
    dmid,
    dlow,
    tokens,
    gains,
    cosine,
    sine,
    w_out,
    own,
    other,
    qkv,
    u,
    lse,
    small,
):
    rows = SLOT_ROWS
    half = MODEL_WIDTH // 2
    middle = KEY_VALUE_HEADS // 2
    return pl.pallas_call(
        backward_kernel,
        grid_spec=pltpu.PrefetchScalarGridSpec(
            num_scalar_prefetch=1,
            grid=(KEY_VALUE_HEADS,),
            in_specs=[
                resident((rows, MODEL_WIDTH)),
                resident((rows, MODEL_WIDTH)),
                resident((rows, MODEL_WIDTH)),
                resident((1, GN)),
                resident((rows, HEAD_SIZE)),
                resident((rows, HEAD_SIZE)),
                pl.BlockSpec((256, MODEL_WIDTH), lambda g, _: (g, 0)),
                pl.BlockSpec((1, half, 512), lambda g, _: (g, 0, 0)),
                pl.BlockSpec((1, half, 512), lambda g, _: (g, 0, 0)),
                pl.BlockSpec((1, rows, 512), lambda g, _: (g, 0, 0)),
                pl.BlockSpec((1, rows, 384), lambda g, _: (g, 0, 0)),
                pl.BlockSpec((1, rows, 256), lambda g, _: (g, 0, 0)),
                resident((8, MODEL_WIDTH)),
            ],
            out_specs=[
                whole((rows, MODEL_WIDTH)),
                pl.BlockSpec((rows, 256), lambda g, _: (0, jnp.minimum(g, middle - 1))),
                pl.BlockSpec((rows, 256), lambda g, _: (0, jnp.maximum(g - middle, 0))),
                pl.BlockSpec((rows, 128), lambda g, _: (0, g)),
                pl.BlockSpec((rows, 128), lambda g, _: (0, g)),
                whole((8, MODEL_WIDTH)),
            ],
            scratch_shapes=[
                pltpu.VMEM((rows, half), F32),
                pltpu.VMEM((rows, half), F32),
                pltpu.VMEM((8, HEAD_SIZE), F32),
                pltpu.VMEM((rows, HEAD_SIZE), F32),
                pltpu.VMEM((rows, HEAD_SIZE), F32),
            ],
        ),
        out_shape=[shape_of((rows, MODEL_WIDTH), BF)]
        + [shape_of((rows, 1024), BF)] * 4
        + [shape_of((8, MODEL_WIDTH), F32)],
        compiler_params=params(),
        name="backward",
    )(meta, dmid, dlow, tokens, gains, cosine, sine, w_out, own, other, qkv, u, lse, small)


def store_pieces(acc, rank, pieces, targets):
    piece = acc.shape[0] // pieces
    share = pieces // len(targets)
    for at in range(pieces):
        source = pl.multiple_of(lax.bitwise_xor(at, rank) * piece, piece)
        place = at % share
        targets[at // share][place * piece : (place + 1) * piece, :] = low(
            acc[pl.ds(source, piece), :]
        )


def quarters(rows, columns):
    return [shape_of((rows // 4, columns), BF)] * 4


def grad_in_kernel(meta_ref, *refs, route, lefts, spans):
    sources, (*targets, acc) = refs[: 2 * (lefts + len(spans))], refs[2 * (lefts + len(spans)) :]
    step = pl.program_id(0)
    for at, (left, start, stop, _) in enumerate(spans):
        l_own, l_got = sources[2 * left : 2 * left + 2]
        r_own, r_got = sources[2 * (lefts + at) : 2 * (lefts + at) + 2]

        @pl.when((step >= start) & (step < stop))
        def _():
            acc[...] = mul_at(l_own[...], r_own[...]) + mul_at(l_got[...], r_got[...])

    store_pieces(acc, meta_ref[route.slot], route.pieces, targets)


def grad_in(meta, lefts, rights, route, block=1024):
    tokens, rows = lefts[0][0].shape
    spans, count = [], 0
    for left, _, _, first, blocks in rights:
        spans.append((left, count, count + blocks, first))
        count += blocks
    outs = quarters(rows, count * block)
    out = pl.BlockSpec((outs[0].shape[0], block), lambda j, _: (0, j))

    def right_spec(start, stop, first):
        return pl.BlockSpec(
            (tokens, block), lambda j, _: (0, first + jnp.clip(j, start, stop - 1) - start)
        )

    return pl.pallas_call(
        functools.partial(grad_in_kernel, route=route, lefts=len(lefts), spans=spans),
        grid_spec=pltpu.PrefetchScalarGridSpec(
            num_scalar_prefetch=1,
            grid=(count,),
            in_specs=[resident((tokens, rows))] * (2 * len(lefts))
            + [right_spec(*span[1:]) for span in spans for _ in range(2)],
            out_specs=[out] * len(outs),
            scratch_shapes=[pltpu.VMEM((rows, block), F32)],
        ),
        out_shape=outs,
        compiler_params=params(),
        name="grad_in",
    )(meta, *(v for left in lefts for v in left), *(v for right in rights for v in right[1:3]))


def grad_out_kernel(
    meta_ref, l_own, l_got, d_own, d_got, e_own, e_got, *targets, route
):
    *targets, acc = targets
    attended = QUERY_HEADS * HEAD_SIZE
    acc[attended:, :] = mul_at(l_own[:, attended:], e_own[...]) + mul_at(
        l_got[:, attended:], e_got[...]
    )

    def upper(own, got):
        for at in range(0, attended, 512):
            rows = slice(at, at + 512)
            acc[rows, :] = mul_at(l_own[:, rows], own) + mul_at(l_got[:, rows], got)

    @pl.when(meta_ref[0] == 0)
    def _():
        upper(d_own[...], d_got[...])

    @pl.when(meta_ref[0] != 0)
    def _():
        upper(e_own[...], e_got[...])

    store_pieces(acc, meta_ref[route.slot], route.pieces, targets)


def grad_out(meta, l_own, got, d_own, e_own, e_got, route):
    tokens, rows = l_own.shape
    block = 512
    outs = quarters(rows, MODEL_WIDTH)
    left = resident((tokens, rows))
    right = pl.BlockSpec((tokens, block), lambda j, _: (0, j))
    out = pl.BlockSpec((outs[0].shape[0], block), lambda j, _: (0, j))
    return pl.pallas_call(
        functools.partial(grad_out_kernel, route=route),
        grid_spec=pltpu.PrefetchScalarGridSpec(
            num_scalar_prefetch=1,
            grid=(MODEL_WIDTH // block,),
            in_specs=[
                left,
                left,
                right,
                pl.BlockSpec((tokens, block), lambda j, _: (0, rows // block + j)),
                right,
                right,
            ],
            out_specs=[out] * len(outs),
            scratch_shapes=[pltpu.VMEM((rows, block), F32)],
        ),
        out_shape=outs,
        compiler_params=params(),
        name="grad_out",
    )(meta, l_own, got, d_own, got, e_own, e_got)


class Route:
    def __init__(self, slot, bits, chips, cores):
        self.slot, self.chips, self.cores = slot, chips, cores
        even = list(bits)
        crossed = {0: 1, 1: 0}
        self.orders = [even, [crossed.get(bit, bit) for bit in even]]
        self.stages = len(even)
        self.pieces = 1 << self.stages
        self.groups = {}
        for chip in range(chips):
            for core in range(cores):
                kept = sum(1 << bit for bit in self.orders[core % 2])
                self.groups.setdefault((core, chip & kept), []).append(chip * cores + core)
        self.groups = list(self.groups.values())
        self.whole = len(self.groups) == chips * cores

    def rank(self, chip, core):
        def code(order):
            value = 0
            for bit in order:
                value = 2 * value + ((chip >> bit) & 1)
            return value

        return jnp.where(core % 2 == 0, code(self.orders[0]), code(self.orders[1]))

    def swap(self, values, stage):
        pairs = [
            (
                chip * self.cores + core,
                (chip ^ (1 << self.orders[core % 2][stage])) * self.cores + core,
            )
            for chip in range(self.chips)
            for core in range(self.cores)
        ]
        return lax.ppermute(values, ("dp", "shard"), pairs)


class Line:
    def __init__(self):
        self.last = None

    def __call__(self, operation, *operands):
        if self.last is not None:
            operands = lax.optimization_barrier((*operands, self.last))[:-1]
        result = operation(*operands)
        self.last = result[0] if isinstance(result, (tuple, list)) else result
        return result


class Sum:
    def __init__(self, line, route, name):
        self.line, self.route, self.name = line, route, name

    def swap(self, values, stage, what):
        with jax.named_scope(f"{self.name}_{what}_{stage}"):
            return self.route.swap(values, stage)

    def begin(self, operation, *operands):
        *self.keeps, send, first = self.line(operation, *operands)
        self.first_got = self.swap(first, 0, "halving_first")
        self.got = self.swap(send, 0, "halving")
        self.stage = 0

    def add_sent(self):
        send = self.line(lambda a, b: low(wide(a) + wide(b)), self.keeps[1], self.first_got)
        self.next_got = self.swap(send, 1, "halving")

    def add_kept(self):
        self.keep = self.line(lambda a, b: low(wide(a) + wide(b)), self.keeps[0], self.got)
        self.got, self.stage = self.next_got, 1

    def add(self):
        half = self.keep.shape[0] // 2
        if self.stage == self.route.stages - 1:
            self.mine = self.line(lambda a, b: low(wide(a) + wide(b)), self.keep, self.got)
            if self.route.whole:
                self.got = self.swap(self.mine, self.stage, "doubling")
            else:
                with jax.named_scope(f"{self.name}_rest"):
                    self.mine = lax.psum(
                        self.mine, ("dp", "shard"), axis_index_groups=self.route.groups
                    )
            return
        send = self.line(lambda a, b: low(wide(a[half:]) + wide(b[half:])), self.keep, self.got)
        self.stage += 1
        got = self.swap(send, self.stage, "halving")
        self.keep = self.line(lambda a, b: low(wide(a[:half]) + wide(b[:half])), self.keep, self.got)
        self.got = got

    def back(self):
        self.mine = lax.optimization_barrier((self.mine, self.line.last))[0]
        self.got = self.swap(self.mine, 1, "doubling")
        self.far = [self.swap(self.mine, 0, "doubling")]

    def join(self):
        if self.stage > 1:
            self.mine = self.line(
                lambda a, b: jnp.concatenate([a, b], axis=0), self.mine, self.got
            )
            self.stage -= 1
            self.got = self.swap(self.mine, self.stage, "doubling")
            if self.stage == 1:
                self.far = [self.swap(self.mine, 0, "doubling")]
        else:
            self.got = lax.optimization_barrier((self.got, self.line.last))[0]
            self.far.append(self.swap(self.got, 0, "doubling_last"))
            self.near = [self.mine, self.got]


def adam(weight, first, second, gradient, rate, decay):
    first = BETA_ONE * first + (1.0 - BETA_ONE) * gradient
    second = BETA_TWO * second + ((1.0 - BETA_TWO) * gradient) * gradient
    square = second * (1.0 / (1.0 - BETA_TWO**STEP))
    root = square * lax.rsqrt(square) + ADAM_EPSILON
    step = (first * (rate / (1.0 - BETA_ONE**STEP))) / root
    return weight * (1.0 - rate * decay) - step, first, second


def adam_kernel(meta_ref, *refs, route, joint, parts):
    pairs = [refs[2 * at : 2 * at + 2] for at in range(parts)]
    w_ref, f_ref, s_ref = refs[2 * parts : 2 * parts + 3]
    new_w, new_f, new_s = refs[-3:]
    pieces = route.pieces // 2 if joint else route.pieces // 4
    piece = w_ref.shape[0] // pieces
    inner = lax.rem(meta_ref[route.slot], pieces)
    share = route.pieces // 4

    def update(*g_refs):
        for at in range(pieces):
            source = pl.multiple_of(lax.bitwise_xor(at, inner) % share * piece, piece)
            there = slice(at * piece, (at + 1) * piece)
            new_w[there, :], new_f[there, :], new_s[there, :] = adam(
                w_ref[there, :],
                f_ref[there, :],
                s_ref[there, :],
                wide(g_refs[at // share][pl.ds(source, piece), :]),
                MATRIX_RATE,
                MATRIX_DECAY,
            )

    step = pl.program_id(0)
    for at, (near, far) in enumerate(pairs):
        now = (step if joint else step // 2) == at
        near_first = inner < share if joint else step % 2 == 0

        @pl.when(now & near_first)
        def _():
            update(near, far)

        @pl.when(now & jnp.logical_not(near_first))
        def _():
            update(far, near)


def adam_call(meta, route, gradients, states, done, block, place, part, joint):
    rows, columns = gradients[0].shape
    parts = len(gradients) // 2
    steps = 1 if joint else 2
    tall = rows * 2 // steps
    last = columns // block - 1

    def g_spec(at):
        first = at // 2 if joint else at
        return pl.BlockSpec(
            (rows, block),
            lambda t, j, m: (0, jnp.where(t == first, j, jnp.where(t < first, 0, last))),
        )

    spec = pl.BlockSpec(
        (tall, block),
        lambda t, j, m: (
            lax.bitwise_xor(t + part * steps, m[route.slot] // (route.pieces // (2 * steps))),
            place(j),
        ),
    )
    return pl.pallas_call(
        functools.partial(adam_kernel, route=route, joint=joint, parts=parts),
        grid_spec=pltpu.PrefetchScalarGridSpec(
            num_scalar_prefetch=1,
            grid=(parts * steps, columns // block),
            in_specs=[g_spec(at) for at in range(2 * parts)]
            + [spec, spec, spec]
            + [pl.BlockSpec(memory_space=pl.ANY)] * len(done),
            out_specs=[spec, spec, spec],
        ),
        out_shape=[shape_of(states[0].shape, F32)] * 3,
        input_output_aliases={4 + 2 * parts + i: i for i in range(len(done))},
        compiler_params=params(2),
        name="adam",
    )(meta, *gradients, *states, *done)


def rope_constants():
    index = np.arange(HEAD_SIZE // 2, dtype=np.float32)
    frequency = np.exp(index * np.float32(-2.0 * math.log(1000000.0) / HEAD_SIZE))
    angles = np.arange(SLOT_ROWS, dtype=np.float32)[:, None] * frequency[None, :]
    cosine, sine = np.cos(angles), np.sin(angles)
    return (
        np.concatenate([cosine, cosine], axis=1).astype(np.float32),
        np.concatenate([-sine, sine], axis=1).astype(np.float32),
    )


def core_swap(values):
    return lax.ppermute(values, "shard", [(0, 1), (1, 0)])


SUM_ROUTES = (0, 1, 3)

SCHEDULE = (
    "out", "mix", "out>", "K", "small", "mix>", "out*", "mix*", "out+", "mix+", "qkv",
    "out+", "mix+", "qkv>", "mix+", "out+", "mix=", "qkv*", "out=", "small+", "qkv+",
    "small+", "mix=", "out=", "small+", "mix=", "mix!0", "small+", "out=", "out!0", "qkv-",
    "mix!1", "out!1", "qkv=", "qkv!0", "small+", "qkv!1",
)


def slot_shards(
    tokens,
    cotangent,
    lengths,
    w_in,
    w_out,
    gains,
    first_in,
    first_out,
    gain_first,
    second_in,
    second_out,
    gain_second,
):
    chip, core = lax.axis_index("dp"), lax.axis_index("shard")
    chips, cores = lax.axis_size("dp"), lax.axis_size("shard")
    routes = [
        Route(2, (0, 2, 1, 3), chips, cores),
        Route(3, (0, 1, 2, 3), chips, cores),
        Route(4, (0, 2), chips, cores),
        Route(5, (0, 1), chips, cores),
    ]
    meta = jnp.stack([core, lengths[0]] + [r.rank(chip, core) for r in routes]).astype(jnp.int32)
    line = Line()

    gains_own = low(gains).reshape(1, -1)
    gains_other = core_swap(gains_own)
    out_all = lax.all_gather(
        line(lambda v: cast_rows(v, 640), w_out), "shard", axis=0, tiled=True
    )
    gain_all = line(lambda a, b: wide(join_columns(a, b, core)), gains_own, gains_other)
    valid = lax.broadcasted_iota(jnp.int32, (SLOT_ROWS, 1), 0) < lengths[0]
    e = line(lambda v: jnp.where(valid, v, jnp.zeros((), BF)), cotangent)
    e_got = core_swap(e)
    qkv_own = line(cast_qkv, w_in)
    qkv_other = core_swap(qkv_own)
    mix_own = line(cast_mix, w_in)
    mix_other = [core_swap(rows) for rows in mix_own]
    cosine, sine = (jnp.asarray(table) for table in rope_constants())

    o, qkv, u, lse, a_own, a_other = line(
        forward,
        meta,
        tokens,
        gain_all,
        cosine,
        sine,
        qkv_own,
        qkv_other,
    )
    a_got = core_swap(a_other)
    o, e_got, a_got = lax.optimization_barrier((o, e_got, a_got))
    y, dgate, dup, b_own, b_other, left, send, dmid, dlow, small = line(
        unit, meta, o, tokens, e, gain_all, out_all, *mix_own, *mix_other
    )
    left_got, b_got = core_swap(send), core_swap(b_other)
    dgate_got, dup_got = core_swap(dgate), core_swap(dup)

    out, mix, qkv_sum = (
        Sum(line, routes[at], name) for at, name in zip(SUM_ROUTES, ("out", "mix", "qkv"))
    )
    states_in = (w_in, first_in, second_in)
    states_out = (w_out, first_out, second_out)
    now = {"in": (), "out": (), "small": small}
    back_inputs = (
        meta, dmid, dlow, tokens, gain_all, cosine, sine, out_all, qkv_own, qkv_other, qkv, u, lse, small,
    )

    def heads():
        now["dx"], *du, now["small"] = line(backward, *back_inputs)
        now["du"] = [(own, core_swap(own)) for own in du]

    def small_start():
        now["small_got"] = core_swap(now["small"])
        now["stage"] = 0

    def small_next():
        now["small"] = line(lambda a, b: a + b, now["small"], now["small_got"])
        if now["stage"] < 4:
            now["small_got"] = routes[1].swap(now["small"], now["stage"])
            now["stage"] += 1

    def begin_in(total, lefts, rights):
        spans = [(left, first, count) for left, _, _, first, count in rights]
        operands = [v for pair in lefts for v in pair] + [v for right in rights for v in right[1:3]]

        def operation(*o):
            pairs = list(zip(o[::2], o[1::2]))
            return grad_in(
                meta,
                pairs[: len(lefts)],
                [
                    (left, *pair, first, count)
                    for pair, (left, first, count) in zip(pairs[len(lefts) :], spans)
                ],
                total.route,
            )

        total.begin(operation, *operands)

    def begin_mix():
        begin_in(
            mix,
            [(b_own, b_got)],
            [(0, dgate, dgate_got, 1, 2), (0, dup, dup_got, 0, 3)],
        )

    def begin_qkv():
        begin_in(
            qkv_sum,
            [(a_own, a_got), (b_own, b_got)],
            [(0, own, got, 0, 1) for own, got in now["du"]] + [(1, dgate, dgate_got, 0, 1)],
        )

    def update(total, name, states, block, place, joint, part=None):
        gradients = (total.near if part != 1 else []) + (total.far if part != 0 else [])
        count = len(gradients)
        now[name] = line(
            lambda *o: adam_call(
                meta,
                total.route,
                o[:count],
                o[count : count + 3],
                o[count + 3 :],
                block,
                place,
                part or 0,
                joint,
            ),
            *gradients,
            *states,
            *now[name],
        )

    updates = {
        "mix": functools.partial(update, mix, "in", states_in, 1280, lambda j: 4 + j, True),
        "out": functools.partial(update, out, "out", states_out, 512, lambda j: j, False),
        "qkv": functools.partial(update, qkv_sum, "in", states_in, 1280, lambda j: j, True),
    }
    steps = {
        "mix": begin_mix,
        "out": lambda: out.begin(
            lambda *o: grad_out(meta, *o, out.route), left, left_got, dlow, e, e_got
        ),
        "qkv": begin_qkv,
        "K": heads,
        "small": small_start,
        "small+": small_next,
    }
    for name, total in (("mix", mix), ("out", out), ("qkv", qkv_sum)):
        steps[name + ">"] = total.add_sent
        steps[name + "*"] = total.add_kept
        steps[name + "+"] = total.add
        steps[name + "-"] = total.back
        steps[name + "="] = total.join
        steps[name + "!"] = updates[name]
        for part in range(2):
            steps[name + "!" + str(part)] = functools.partial(updates[name], part=part)
    for step in SCHEDULE:
        steps[step]()

    small = now["small"]
    valid_rms = jnp.sqrt(
        jnp.stack([small[3, 0], small[2, 512]]) / (small[4, 0] * MODEL_WIDTH)
    )
    gain_sum = lax.dynamic_slice_in_dim(
        jnp.concatenate([small[0], small[1], small[2, :256]]), core * gains.shape[0], gains.shape[0]
    )
    new_gains, new_gain_first, new_gain_second = adam(
        gains, gain_first, gain_second, gain_sum, GAIN_RATE, 0.0
    )
    return (
        y,
        now["dx"],
        now["in"][0],
        now["out"][0],
        new_gains,
        now["in"][1],
        now["out"][1],
        new_gain_first,
        now["in"][2],
        now["out"][2],
        new_gain_second,
        valid_rms,
    )


def solution(mesh):
    in_specs = (
        P(("dp", "shard"), None),
        P(("dp", "shard"), None),
        P(("dp", "shard")),
        P("shard", None),
        P("shard", None),
        P("shard"),
        P("shard", None),
        P("shard", None),
        P("shard"),
        P("shard", None),
        P("shard", None),
        P("shard"),
    )
    out_specs = (
        P(("dp", "shard"), None),
        P(("dp", "shard"), None),
        P("shard", None),
        P("shard", None),
        P("shard"),
        P("shard", None),
        P("shard", None),
        P("shard"),
        P("shard", None),
        P("shard", None),
        P("shard"),
        P(),
    )
    chips, cores = mesh.shape["dp"], mesh.shape["shard"]
    program = slot_shards if cores == 2 and chips == 16 else shards
    return jax.shard_map(program, mesh=mesh, in_specs=in_specs, out_specs=out_specs, check_vma=False)
```

profile of v0, /device:TPU:0, one launch (start us, length us, event | category | flops | bytes accessed | tf_op | source)
XLA Modules:
  0.0 457.5 jit_solution(4401044758949889854)
XLA Ops:
  7.2 6.5 %cast_out.1 = bf16[2560,1024]{1,0:T(8,128)(2,1)} custom-call(f32[2560,1024]{1,0:T(8,128)} %refs_2_.3), custom_call_target="tpu_custom_call" | custom-call | tf_op jit(solution)/shard_map/cast_out/pallas_call | solution.py:414
  17.6 5.7 %cast_qkv.1.own_ref = bf16[8,512,512]{2,1,0:T(8,128)(2,1)} custom-call(f32[512,10240]{1,0:T(8,128)} %refs_2_.5, f32[512,10240]{1,0:T(8,128)} %refs_2_.5, f32[512,10240]{1,0:T(8,128)} %refs_2_.5), custom_call_target="tpu_custom_call" | custom-call | tf_op jit(solution)/shard_map/cast_qkv/pallas_call | solution.py:392
  23.6 10.2 %cast_mix.1 = (bf16[3,256,2048]{2,1,0:T(8,128)(2,1)}, bf16[3,256,2048]{2,1,0:T(8,128)(2,1)}) custom-call(f32[512,10240]{1,0:T(8,128)} %refs_2_.5, f32[512,10240]{1,0:T(8,128)} %refs_2_.5), custom_call_target="tpu_custom_call" | custom-call | tf_op jit(solution)/shard_map/cast_mix/pallas_call | solution.py:439
  35.1 23.7 %forward.1 = (bf16[512,2048]{1,0:T(8,128)(2,1)}, bf16[8,512,512]{2,1,0:T(8,128)(2,1)}, f32[8,512,384]{2,1,0:T(8,128)}, f32[8,512,256]{2,1,0:T(8,128)}, bf16[512,...) custom-call(s32[6]{0:T(128)} %stack.26.meta_ref, bf16[512,1024]{1,0:T(8,128)(2,1)} %x_ref.2, ...), custom_call_target="tpu_custom_call" | custom-call | tf_op jit(solution)/shard_map/forward/pallas_call | solution.py:534
  61.2 39.0 %unit.1 = (bf16[512,1024]{1,0:T(8,128)(2,1)}, bf16[512,3072]{1,0:T(8,128)(2,1)}, bf16[512,3072]{1,0:T(8,128)(2,1)}, bf16[512,512]{1,0:T(8,128)(2,1)}, bf16[512,5...) custom-call(s32[6]{0:T(128)} %stack.26.meta_ref, ...), custom_call_target="tpu_custom_call" | custom-call | tf_op jit(solution)/shard_map/unit/pallas_call | solution.py:693
  101.3 5.7 %collective-permute-done.6.l_got.d_got = bf16[512,3584]{1,0:T(8,128)(2,1)} collective-permute-done((bf16[512,3584]{1,0:T(8,128)(2,1)}, bf16[512,3584]{1,0:T(8,128)(2,1)}, u32[]{:S(2)}, u32[]{:S(2)}) %collective-permute-start.6) | collective-permute-done | bytes 3670048 | tf_op jit(solution)/shard_map/ppermute | solution.py:1245
  107.0 12.7 %grad_out.1 = (bf16[640,1024]{1,0:T(8,128)(2,1)}, bf16[640,1024]{1,0:T(8,128)(2,1)}, bf16[640,1024]{1,0:T(8,128)(2,1)}, bf16[640,1024]{1,0:T(8,128)(2,1)}) custom-call(s32[6]{0:T(128)} %stack.26.meta_ref, bf16[512,2560]{1,0:T(8,128)(2,1)} %get-tuple-element.265.l_own, bf16[512,3584]{1,0:T(8,128)(2,1)} %collective-permute-done.6.l_got.d_got, ...), custom_call_target="tpu_custom_call" | custom-call | tf_op jit(solution)/shard_map/grad_out/pallas_call | solution.py:1019
  122.4 12.2 %grad_in.2 = (bf16[128,5120]{1,0:T(8,128)(2,1)}, bf16[128,5120]{1,0:T(8,128)(2,1)}, bf16[128,5120]{1,0:T(8,128)(2,1)}, bf16[128,5120]{1,0:T(8,128)(2,1)}) custom-call(s32[6]{0:T(128)} %stack.26.meta_ref, bf16[512,512]{1,0:T(8,128)(2,1)} %get-tuple-element.327.refs_0_.refs_2_, bf16[512,512]{1,0:T(8,128)(2,1)} %collective-permute-done.8.refs_1_.refs_3_, ...), custom_call_target="tpu_custom_call" | custom-call | tf_op jit(solution)/shard_map/grad_in/pallas_call | solution.py:971
  143.8 40.5 %backward.1 = (bf16[512,1024]{1,0:T(8,128)(2,1)}, bf16[512,1024]{1,0:T(8,128)(2,1)}, bf16[512,1024]{1,0:T(8,128)(2,1)}, bf16[512,1024]{1,0:T(8,128)(2,1)}, bf16[512,1024]{1,0:T(8,128)(2,1)}, /*index=5*/f32[8,1024]{1,0:T(8,128)}) custom-call(s32[6]{0:T(128)} %stack.26.meta_ref, f32[512,1024]{1,0:T(8,128)} %get-tuple-element.287.dmid_ref, ...), custom_call_target="tpu_custom_call" | custom-call | tf_op jit(solution)/shard_map/backward/pallas_call | solution.py:884
  197.2 7.0 %collective-permute-done.18 = bf16[128,5120]{1,0:T(8,128)(2,1)S(1)} collective-permute-done((bf16[128,5120]{1,0:T(8,128)(2,1)S(1)}, bf16[128,5120]{1,0:T(8,128)(2,1)S(1)}, u32[]{:S(2)}, u32[]{:S(2)}) %collective-permute-start.18) | collective-permute-done | bytes 1310752 | tf_op jit(solution)/shard_map/mix_halving_1/ppermute | solution.py:1075
  210.4 13.5 %grad_in.3 = (bf16[128,5120]{1,0:T(8,128)(2,1)}, bf16[128,5120]{1,0:T(8,128)(2,1)}, bf16[128,5120]{1,0:T(8,128)(2,1)}, bf16[128,5120]{1,0:T(8,128)(2,1)}) custom-call(s32[6]{0:T(128)} %stack.26.meta_ref, bf16[512,512]{1,0:T(8,128)(2,1)} %get-tuple-element.325.refs_0_, bf16[512,512]{1,0:T(8,128)(2,1)} %collective-permute-done.3.refs_1_, ...), custom_call_target="tpu_custom_call" | custom-call | tf_op jit(solution)/shard_map/grad_in/pallas_call | solution.py:971
  233.2 8.6 %collective-permute-done.24 = bf16[128,5120]{1,0:T(8,128)(2,1)S(1)} collective-permute-done((bf16[128,5120]{1,0:T(8,128)(2,1)}, bf16[128,5120]{1,0:T(8,128)(2,1)S(1)}, u32[]{:S(2)}, u32[]{:S(2)}) %collective-permute-start.24) | collective-permute-done | bytes 1310752 | tf_op jit(solution)/shard_map/qkv_halving_first_0/ppermute | solution.py:1075
  242.1 13.8 %collective-permute-done.23 = bf16[32,5120]{1,0:T(8,128)(2,1)S(1)} collective-permute-done((bf16[32,5120]{1,0:T(8,128)(2,1)S(1)}, bf16[32,5120]{1,0:T(8,128)(2,1)S(1)}, u32[]{:S(2)}, u32[]{:S(2)}) %collective-permute-start.23) | collective-permute-done | bytes 327712 | tf_op jit(solution)/shard_map/mix_halving_3/ppermute | solution.py:1075
  260.2 21.5 %collective-permute-done.25 = bf16[32,5120]{1,0:T(8,128)(2,1)S(1)} collective-permute-done((bf16[32,5120]{1,0:T(8,128)(2,1)S(1)}, bf16[32,5120]{1,0:T(8,128)(2,1)S(1)}, u32[]{:S(2)}, u32[]{:S(2)}) %collective-permute-start.25) | collective-permute-done | bytes 327712 | tf_op jit(solution)/shard_map/mix_doubling_3/ppermute | solution.py:1075
  292.5 8.2 %collective-permute-done.31 = bf16[64,5120]{1,0:T(8,128)(2,1)S(1)} collective-permute-done((bf16[64,5120]{1,0:T(8,128)(2,1)S(1)}, bf16[64,5120]{1,0:T(8,128)(2,1)S(1)}, u32[]{:S(2)}, u32[]{:S(2)}) %collective-permute-start.31) | collective-permute-done | bytes 655392 | tf_op jit(solution)/shard_map/mix_doubling_2/ppermute | solution.py:1075
  306.4 14.2 %collective-permute-done.34 = f32[8,1024]{1,0:T(8,128)S(1)} collective-permute-done((f32[8,1024]{1,0:T(8,128)S(1)}, f32[8,1024]{1,0:T(8,128)S(1)}, u32[]{:S(2)}, u32[]{:S(2)}) %collective-permute-start.34) | collective-permute-done | bytes 32800 | tf_op jit(solution)/shard_map/ppermute | solution.py:1075
  323.8 13.1 %adam.6 = (f32[512,10240]{1,0:T(8,128)}, f32[512,10240]{1,0:T(8,128)}, f32[512,10240]{1,0:T(8,128)}) custom-call(s32[6]{0:T(128)} %stack.26.meta_ref, bf16[128,5120]{1,0:T(8,128)(2,1)} %constant_dynamic-update-slice_fusion.4.refs_0_, bf16[128,5120]{1,0:T(8,128)(2,1)} %collective-permute-done.36.refs_1_, f32[512,10240]{1,0:T(8,128)} %refs_2_.5, ...), custom_call_target="tpu_custom_call" | custom-call | tf_op jit(solution)/shard_map/adam/pallas_call | solution.py:1216
  336.9 20.4 %collective-permute-done.35 = f32[8,1024]{1,0:T(8,128)} collective-permute-done((f32[8,1024]{1,0:T(8,128)}, f32[8,1024]{1,0:T(8,128)}, u32[]{:S(2)}, u32[]{:S(2)}) %collective-permute-start.35) | collective-permute-done | bytes 32800 | tf_op jit(solution)/shard_map/ppermute | solution.py:1075
  360.2 13.1 %adam.7 = (f32[2560,1024]{1,0:T(8,128)}, f32[2560,1024]{1,0:T(8,128)}, f32[2560,1024]{1,0:T(8,128)}) custom-call(s32[6]{0:T(128)} %stack.26.meta_ref, bf16[640,1024]{1,0:T(8,128)(2,1)} %constant_dynamic-update-slice_fusion.6.refs_0_, bf16[640,1024]{1,0:T(8,128)(2,1)} %collective-permute-done.33.refs_1_, f32[2560,1024]{1,0:T(8,128)} %refs_2_.3, ...), custom_call_target="tpu_custom_call" | custom-call | tf_op jit(solution)/shard_map/adam/pallas_call | solution.py:1216
  373.3 11.3 %all-reduce.2.cloned.1.call-done.refs_0_ = bf16[128,5120]{1,0:T(8,128)(2,1)} async-done(((bf16[128,5120]{1,0:T(8,128)(2,1)}), bf16[128,5120]{1,0:T(8,128)(2,1)}) %all-reduce.2.cloned.1.call-update) | async-done | bytes 1310736 | tf_op jit(solution)/shard_map/qkv_rest/psum | solution.py:1120
  387.6 12.9 %adam.8 = (f32[512,10240]{1,0:T(8,128)}, f32[512,10240]{1,0:T(8,128)}, f32[512,10240]{1,0:T(8,128)}) custom-call(s32[6]{0:T(128)} %stack.26.meta_ref, bf16[128,5120]{1,0:T(8,128)(2,1)} %collective-permute-done.41.refs_0_, bf16[128,5120]{1,0:T(8,128)(2,1)} %collective-permute-done.42.refs_1_, ...), custom_call_target="tpu_custom_call", output_to_operand_aliasing={{0}: (6, {}), {1}: (7, {}), {2}: (8, {})} | custom-call | tf_op jit(solution)/shard_map/adam/pallas_call | solution.py:1216
  400.5 12.9 %adam.9 = (f32[2560,1024]{1,0:T(8,128)}, f32[2560,1024]{1,0:T(8,128)}, f32[2560,1024]{1,0:T(8,128)}) custom-call(s32[6]{0:T(128)} %stack.26.meta_ref, bf16[640,1024]{1,0:T(8,128)(2,1)} %collective-permute-done.39.refs_0_, bf16[640,1024]{1,0:T(8,128)(2,1)} %collective-permute-done.40.refs_1_, ...), custom_call_target="tpu_custom_call", output_to_operand_aliasing={{0}: (6, {}), {1}: (7, {}), {2}: (8, {})} | custom-call | tf_op jit(solution)/shard_map/adam/pallas_call | solution.py:1216
  419.3 12.9 %adam.10 = (f32[512,10240]{1,0:T(8,128)}, f32[512,10240]{1,0:T(8,128)}, f32[512,10240]{1,0:T(8,128)}) custom-call(s32[6]{0:T(128)} %stack.26.meta_ref, bf16[128,5120]{1,0:T(8,128)(2,1)} %all-reduce.2.cloned.1.call-done.refs_0_, bf16[128,5120]{1,0:T(8,128)(2,1)} %collective-permute-done.38.refs_1_, ...), custom_call_target="tpu_custom_call", output_to_operand_aliasing={{0}: (6, {}), {1}: (7, {}), {2}: (8, {})} | custom-call | tf_op jit(solution)/shard_map/adam/pallas_call | solution.py:1216
  437.6 12.9 %adam.11 = (f32[512,10240]{1,0:T(8,128)}, f32[512,10240]{1,0:T(8,128)}, f32[512,10240]{1,0:T(8,128)}) custom-call(s32[6]{0:T(128)} %stack.26.meta_ref, bf16[128,5120]{1,0:T(8,128)(2,1)} %collective-permute-done.37.refs_0_, bf16[128,5120]{1,0:T(8,128)(2,1)} %collective-permute-done.43.refs_1_, ...), custom_call_target="tpu_custom_call", output_to_operand_aliasing={{0}: (6, {}), {1}: (7, {}), {2}: (8, {})} | custom-call | tf_op jit(solution)/shard_map/adam/pallas_call | solution.py:1216
  (163 shorter events, 88.6 us)
Async XLA Ops:
  7.2 54.0 %all-gather.2.cloned.1.call-start = ((), (), s32[]{:S(2)}) async-start(), calls=%async_computation | async-start | bytes 15728640 | tf_op jit(solution)/shard_map/all_gather | solution.py:1285
  13.8 370.9 %all-reduce.2.cloned.1.call-start = ((), (), s32[]{:S(2)}) async-start(), calls=%async_computation.1 | async-start | bytes 2621440 | tf_op jit(solution)/shard_map/qkv_rest/psum | solution.py:1120
  33.9 27.3 %collective-permute-start.4 = (bf16[3,256,2048]{2,1,0:T(8,128)(2,1)}, bf16[3,256,2048]{2,1,0:T(8,128)(2,1)}, u32[]{:S(2)}, u32[]{:S(2)}) collective-permute-start(bf16[3,256,2048]{2,1,0:T(8,128)(2,1)} %get-tuple-element.251.own_top_ref), channel_id=1, source_target_pairs={{0,1},{1,0},{2,3},{3,2},{4,5},{5,4},{6,7},{7,6},{8,9},{9,8},{10,11... | collective-permute-start | bytes 9437192 | tf_op jit(solution)/shard_map/ppermute | solution.py:1245
  34.0 27.1 %collective-permute-start.5 = (bf16[3,256,2048]{2,1,0:T(8,128)(2,1)}, bf16[3,256,2048]{2,1,0:T(8,128)(2,1)}, u32[]{:S(2)}, u32[]{:S(2)}) collective-permute-start(bf16[3,256,2048]{2,1,0:T(8,128)(2,1)} %get-tuple-element.252.own_end_ref), channel_id=1, source_target_pairs={{0,1},{1,0},{2,3},{3,2},{4,5},{5,4},{6,7},{7,6},{8,9},{9,8},{10,11... | collective-permute-start | bytes 9437192 | tf_op jit(solution)/shard_map/ppermute | solution.py:1245
  34.4 24.9 %collective-permute-start.2 = (bf16[512,1024]{1,0:T(8,128)(2,1)}, bf16[512,1024]{1,0:T(8,128)(2,1)}, u32[]{:S(2)}, u32[]{:S(2)}) collective-permute-start(bf16[512,1024]{1,0:T(8,128)(2,1)} %broadcast_select_fusion.e_ref.e_own), channel_id=1, source_target_pairs={{0,1},{1,0},{2,3},{3,2},{4,5},{5,4},{6,7},{7,6},{8,9},{9,8},{10,11... | collective-permute-start | bytes 3145736 | tf_op jit(solution)/shard_map/ppermute | solution.py:1245
  134.6 49.7 %collective-permute-start.17 = (bf16[128,5120]{1,0:T(8,128)(2,1)}, bf16[128,5120]{1,0:T(8,128)(2,1)}, u32[]{:S(2)}, u32[]{:S(2)}) collective-permute-start(bf16[128,5120]{1,0:T(8,128)(2,1)} %get-tuple-element.310), channel_id=1, source_target_pairs={{0,2},{1,5},{2,0},{3,7},{4,6},{5,1},{6,4},{7,3},{8,10},{9,13},{10,... | collective-permute-start | bytes 3932168 | tf_op jit(solution)/shard_map/mix_halving_first_0/ppermute | solution.py:1075
  134.6 53.5 %collective-permute-start.16 = (bf16[640,1024]{1,0:T(8,128)(2,1)}, bf16[640,1024]{1,0:T(8,128)(2,1)}, u32[]{:S(2)}, u32[]{:S(2)}) collective-permute-start(bf16[640,1024]{1,0:T(8,128)(2,1)} %get-tuple-element.308), channel_id=1, source_target_pairs={{0,2},{1,5},{2,0},{3,7},{4,6},{5,1},{6,4},{7,3},{8,10},{9,13},{10,... | collective-permute-start | bytes 3932168 | tf_op jit(solution)/shard_map/out_halving_0/ppermute | solution.py:1075
  136.6 53.3 %collective-permute-start.15 = (bf16[128,5120]{1,0:T(8,128)(2,1)}, bf16[128,5120]{1,0:T(8,128)(2,1)}, u32[]{:S(2)}, u32[]{:S(2)}) collective-permute-start(bf16[128,5120]{1,0:T(8,128)(2,1)} %get-tuple-element.307), channel_id=1, source_target_pairs={{0,2},{1,5},{2,0},{3,7},{4,6},{5,1},{6,4},{7,3},{8,10},{9,13},{10,... | collective-permute-start | bytes 3932168 | tf_op jit(solution)/shard_map/mix_halving_0/ppermute | solution.py:1075
  141.6 50.8 %collective-permute-start.19 = (bf16[640,1024]{1,0:T(8,128)(2,1)}, bf16[640,1024]{1,0:T(8,128)(2,1)}, u32[]{:S(2)}, u32[]{:S(2)}) collective-permute-start(bf16[640,1024]{1,0:T(8,128)(2,1)} %add_convert_fusion.6), channel_id=1, source_target_pairs={{0,8},{1,9},{2,10},{3,11},{4,12},{5,13},{6,14},{7,15},{8,0},{9,1},... | collective-permute-start | bytes 3932168 | tf_op jit(solution)/shard_map/out_halving_1/ppermute | solution.py:1075
  226.7 30.5 %collective-permute-start.26 = (bf16[160,1024]{1,0:T(8,128)(2,1)S(1)}, bf16[160,1024]{1,0:T(8,128)(2,1)S(1)}, u32[]{:S(2)}, u32[]{:S(2)}) collective-permute-start(bf16[160,1024]{1,0:T(8,128)(2,1)S(1)} %add_convert_fusion.16), channel_id=1, source_target_pairs={{0,16},{1,17},{2,18},{3,19},{4,20},{5,21},{6,22},{7,23},{8,24},{9,... | collective-permute-start | bytes 983048 | tf_op jit(solution)/shard_map/out_halving_3/ppermute | solution.py:1075
  231.8 24.2 %collective-permute-start.23 = (bf16[32,5120]{1,0:T(8,128)(2,1)S(1)}, bf16[32,5120]{1,0:T(8,128)(2,1)S(1)}, u32[]{:S(2)}, u32[]{:S(2)}) collective-permute-start(bf16[32,5120]{1,0:T(8,128)(2,1)S(1)} %add_convert_fusion.14), channel_id=1, source_target_pairs={{0,16},{1,17},{2,18},{3,19},{4,20},{5,21},{6,22},{7,23},{8,24},{9,... | collective-permute-start | bytes 983048 | tf_op jit(solution)/shard_map/mix_halving_3/ppermute | solution.py:1075
  256.0 25.7 %collective-permute-start.25 = (bf16[32,5120]{1,0:T(8,128)(2,1)S(1)}, bf16[32,5120]{1,0:T(8,128)(2,1)S(1)}, u32[]{:S(2)}, u32[]{:S(2)}) collective-permute-start(bf16[32,5120]{1,0:T(8,128)(2,1)S(1)} %add_convert_fusion.12), channel_id=1, source_target_pairs={{0,16},{1,17},{2,18},{3,19},{4,20},{5,21},{6,22},{7,23},{8,24},{9,... | collective-permute-start | bytes 983048 | tf_op jit(solution)/shard_map/mix_doubling_3/ppermute | solution.py:1075
  256.1 32.0 %collective-permute-start.28 = (f32[8,1024]{1,0:T(8,128)S(1)}, f32[8,1024]{1,0:T(8,128)S(1)}, u32[]{:S(2)}, u32[]{:S(2)}) collective-permute-start(f32[8,1024]{1,0:T(8,128)S(1)} %copy-done.14), channel_id=1, source_target_pairs={{0,1},{1,0},{2,3},{3,2},{4,5},{5,4},{6,7},{7,6},{8,9},{9,8},{10,11... | collective-permute-start | bytes 98312 | tf_op jit(solution)/shard_map/ppermute | solution.py:1245
  256.2 31.3 %collective-permute-start.20 = (bf16[128,5120]{1,0:T(8,128)(2,1)S(1)}, bf16[128,5120]{1,0:T(8,128)(2,1)S(1)}, u32[]{:S(2)}, u32[]{:S(2)}) collective-permute-start(bf16[128,5120]{1,0:T(8,128)(2,1)S(1)} %copy-done.16), channel_id=1, source_target_pairs={{0,2},{1,5},{2,0},{3,7},{4,6},{5,1},{6,4},{7,3},{8,10},{9,13},{10,... | collective-permute-start | bytes 3932168 | tf_op jit(solution)/shard_map/qkv_halving_0/ppermute | solution.py:1075
  256.7 32.0 %collective-permute-start.27 = (bf16[128,5120]{1,0:T(8,128)(2,1)S(1)}, bf16[128,5120]{1,0:T(8,128)(2,1)S(1)}, u32[]{:S(2)}, u32[]{:S(2)}) collective-permute-start(bf16[128,5120]{1,0:T(8,128)(2,1)S(1)} %add_convert_fusion.2), channel_id=1, source_target_pairs={{0,4},{1,3},{2,6},{3,1},{4,0},{5,7},{6,2},{7,5},{8,12},{9,11},{10,... | collective-permute-start | bytes 3932168 | tf_op jit(solution)/shard_map/qkv_halving_1/ppermute | solution.py:1075
  257.3 30.5 %collective-permute-start.29 = (bf16[160,1024]{1,0:T(8,128)(2,1)S(1)}, bf16[160,1024]{1,0:T(8,128)(2,1)S(1)}, u32[]{:S(2)}, u32[]{:S(2)}) collective-permute-start(bf16[160,1024]{1,0:T(8,128)(2,1)S(1)} %add_convert_fusion.11), channel_id=1, source_target_pairs={{0,16},{1,17},{2,18},{3,19},{4,20},{5,21},{6,22},{7,23},{8,24},{9,... | collective-permute-start | bytes 983048 | tf_op jit(solution)/shard_map/out_doubling_3/ppermute | solution.py:1075
  304.8 53.9 %collective-permute-start.33 = (bf16[640,1024]{1,0:T(8,128)(2,1)}, bf16[640,1024]{1,0:T(8,128)(2,1)}, u32[]{:S(2)}, u32[]{:S(2)}) collective-permute-start(bf16[640,1024]{1,0:T(8,128)(2,1)} %constant_dynamic-update-slice_fusion.6.refs_0_), channel_id=1, source_target_pairs={{0,8},{1,9},{2,10},{3,11},{4,12},{5,13},{6,14},{7,15},{8,0},{9,1},... | collective-permute-start | bytes 3932168 | tf_op jit(solution)/shard_map/out_doubling_1/ppermute | solution.py:1075
  321.3 36.0 %collective-permute-start.35 = (f32[8,1024]{1,0:T(8,128)}, f32[8,1024]{1,0:T(8,128)}, u32[]{:S(2)}, u32[]{:S(2)}) collective-permute-start(f32[8,1024]{1,0:T(8,128)} %add.162), channel_id=1, source_target_pairs={{0,8},{1,9},{2,10},{3,11},{4,12},{5,13},{6,14},{7,15},{8,0},{9,1},... | collective-permute-start | bytes 98312 | tf_op jit(solution)/shard_map/ppermute | solution.py:1075
  321.3 64.8 %collective-permute-start.41 = (bf16[128,5120]{1,0:T(8,128)(2,1)}, bf16[128,5120]{1,0:T(8,128)(2,1)}, u32[]{:S(2)}, u32[]{:S(2)}) collective-permute-start(bf16[128,5120]{1,0:T(8,128)(2,1)} %constant_dynamic-update-slice_fusion.4.refs_0_), channel_id=1, source_target_pairs={{0,2},{1,5},{2,0},{3,7},{4,6},{5,1},{6,4},{7,3},{8,10},{9,13},{10,... | collective-permute-start | bytes 3932168 | tf_op jit(solution)/shard_map/mix_doubling_0/ppermute | solution.py:1075
  321.8 78.7 %collective-permute-start.39 = (bf16[640,1024]{1,0:T(8,128)(2,1)}, bf16[640,1024]{1,0:T(8,128)(2,1)}, u32[]{:S(2)}, u32[]{:S(2)}) collective-permute-start(bf16[640,1024]{1,0:T(8,128)(2,1)} %constant_dynamic-update-slice_fusion.6.refs_0_), channel_id=1, source_target_pairs={{0,2},{1,5},{2,0},{3,7},{4,6},{5,1},{6,4},{7,3},{8,10},{9,13},{10,... | collective-permute-start | bytes 3932168 | tf_op jit(solution)/shard_map/out_doubling_0/ppermute | solution.py:1075
  323.3 64.3 %collective-permute-start.42 = (bf16[128,5120]{1,0:T(8,128)(2,1)}, bf16[128,5120]{1,0:T(8,128)(2,1)}, u32[]{:S(2)}, u32[]{:S(2)}) collective-permute-start(bf16[128,5120]{1,0:T(8,128)(2,1)} %collective-permute-done.36.refs_1_), channel_id=1, source_target_pairs={{0,2},{1,5},{2,0},{3,7},{4,6},{5,1},{6,4},{7,3},{8,10},{9,13},{10,... | collective-permute-start | bytes 3932168 | tf_op jit(solution)/shard_map/mix_doubling_last_0/ppermute | solution.py:1075
  358.7 41.8 %collective-permute-start.40 = (bf16[640,1024]{1,0:T(8,128)(2,1)}, bf16[640,1024]{1,0:T(8,128)(2,1)}, u32[]{:S(2)}, u32[]{:S(2)}) collective-permute-start(bf16[640,1024]{1,0:T(8,128)(2,1)} %collective-permute-done.33.refs_1_), channel_id=1, source_target_pairs={{0,2},{1,5},{2,0},{3,7},{4,6},{5,1},{6,4},{7,3},{8,10},{9,13},{10,... | collective-permute-start | bytes 3932168 | tf_op jit(solution)/shard_map/out_doubling_last_0/ppermute | solution.py:1075
  384.7 32.0 %collective-permute-start.38 = (bf16[128,5120]{1,0:T(8,128)(2,1)}, bf16[128,5120]{1,0:T(8,128)(2,1)}, u32[]{:S(2)}, u32[]{:S(2)}) collective-permute-start(bf16[128,5120]{1,0:T(8,128)(2,1)} %all-reduce.2.cloned.1.call-done.refs_0_), channel_id=1, source_target_pairs={{0,4},{1,3},{2,6},{3,1},{4,0},{5,7},{6,2},{7,5},{8,12},{9,11},{10,... | collective-permute-start | bytes 3932168 | tf_op jit(solution)/shard_map/qkv_doubling_1/ppermute | solution.py:1075
  386.1 51.4 %collective-permute-start.37 = (bf16[128,5120]{1,0:T(8,128)(2,1)}, bf16[128,5120]{1,0:T(8,128)(2,1)}, u32[]{:S(2)}, u32[]{:S(2)}) collective-permute-start(bf16[128,5120]{1,0:T(8,128)(2,1)} %all-reduce.2.cloned.1.call-done.refs_0_), channel_id=1, source_target_pairs={{0,2},{1,5},{2,0},{3,7},{4,6},{5,1},{6,4},{7,3},{8,10},{9,13},{10,... | collective-permute-start | bytes 3932168 | tf_op jit(solution)/shard_map/qkv_doubling_0/ppermute | solution.py:1075
  (40 other events, 478.7 us)
Sparse Core Ops, SparseCore 0:
  13.9 29.8 all-gather.1
  304.9 79.7 all-reduce.1
where the time goes:
time: 462 us; the launch traced here: 458 us
  Pallas kernels  242 us (52%)
  waiting for transfers between devices  126 us (27%)
  starting transfers between devices  36 us (8%)
  other arithmetic  29.9 us (6%)
  between operations  16 us (3%)
  local copies, waits for them, and re-layouts  7.79 us (2%)
    ppermute x30, waiting for transfers between devices, swap(): return lax.ppermute(values, ('dp', 'shard'), pairs)  107 us
    pallas_call x6, Pallas kernels, adam_call(): pl.pallas_call(functools.partial(adam_kernel, route=route, joint=joint, p...  77.9 us
    pallas_call x1, Pallas kernels, backward(): pl.pallas_call(backward_kernel, grid_spec=pltpu.PrefetchScalarGridSpec(nu...  40.5 us
    pallas_call x1, Pallas kernels, unit(): pl.pallas_call(unit_kernel, grid_spec=pltpu.PrefetchScalarGridSpec(num_sc...  39 us
    ppermute x30, starting transfers between devices, swap(): return lax.ppermute(values, ('dp', 'shard'), pairs)  31.8 us
    pallas_call x2, Pallas kernels, grad_in(): pl.pallas_call(functools.partial(grad_in_kernel, route=route, lefts=len(l...  25.7 us
    pallas_call x1, Pallas kernels, forward(): pl.pallas_call(forward_kernel, grid_spec=pltpu.PrefetchScalarGridSpec(num...  23.7 us
    convert_element_type x18, other arithmetic, low(): return values.astype(jnp.bfloat16)  22 us
  transfers between devices with their start and end apart: 47, of which 15 were waited for; matrix products, arithmetic and copies ran while one was open for 8% of the time, Pallas kernels for 40%

commit v1 on v0

--- a/solution.py
+++ b/solution.py
@@ -626,42 +626,40 @@
             send_ref[:, :attended] = o_ref[...]
 
     e = e_ref[...]
-    for part in range(FFB // 512):
-        gates = slice(part * 512, part * 512 + 512)
-        ups = slice(FFB + part * 512, FFB + part * 512 + 512)
-        gate = sum(mul(b_ref[:, rows], w_ref[0, :, gates]) for b_ref, rows, _, w_ref in weights)
-        up = sum(mul(b_ref[:, rows], w_ref[0, :, ups]) for b_ref, rows, _, w_ref in weights)
-        down = wd_ref[gates, :]
-        dh = mul_bt(e, down)
-        sigma = 1.0 / (1.0 + jnp.exp(-gate))
-        silu = gate * sigma
-        hidden = low(silu * up)
-        dgate = low(dh * up * (sigma * (1.0 + gate * (1.0 - sigma))))
-        dup = low(dh * silu)
-        y_s[...] += mul(hidden, down)
-        for _, rows, db_s, w_ref in weights:
-            db_s[:, rows] += mul_bt(dgate, w_ref[0, :, gates]) + mul_bt(dup, w_ref[0, :, ups])
-        dgate_ref[:, gates] = dgate
-        dup_ref[:, gates] = dup
-
-        place = pl.multiple_of(jnp.maximum(step * FFB + part * 512 - 512, 0), 512)
-        first_rows = (step == 0) & (part == 0)
-
-        @pl.when(first_rows & (core == 0))
+    gate = sum(mul(b_ref[:, rows], w_ref[0, :, :FFB]) for b_ref, rows, _, w_ref in weights)
+    up = sum(mul(b_ref[:, rows], w_ref[0, :, FFB:]) for b_ref, rows, _, w_ref in weights)
+    down = wd_ref[...]
+    dh = mul_bt(e, down)
+    sigma = 1.0 / (1.0 + jnp.exp(-gate))
+    silu = gate * sigma
+    hidden = low(silu * up)
+    dgate_ref[...] = low(dh * up * (sigma * (1.0 + gate * (1.0 - sigma))))
+    dup_ref[...] = low(dh * silu)
+    y_s[...] += mul(hidden, down)
+    for _, rows, db_s, w_ref in weights:
+        db_s[:, rows] += mul_bt(dgate_ref[...], w_ref[0, :, :FFB]) + mul_bt(
+            dup_ref[...], w_ref[0, :, FFB:]
+        )
+
+    place = pl.multiple_of(jnp.maximum(step * FFB - 512, 0), 512)
+
+    def place_hidden(first_ref, rest_ref):
+        @pl.when(step == 0)
         def _():
-            left_ref[:, attended:] = hidden
-
-        @pl.when(first_rows & (core != 0))
+            first_ref[:, attended : attended + 512] = hidden[:, :512]
+            rest_ref[:, :512] = hidden[:, 512:]
+
+        @pl.when(step != 0)
         def _():
-            send_ref[:, attended : attended + 512] = hidden
-
-        @pl.when(jnp.logical_not(first_rows) & (core == 0))
-        def _():
-            send_ref[:, pl.ds(place, 512)] = hidden
-
-        @pl.when(jnp.logical_not(first_rows) & (core != 0))
-        def _():
-            left_ref[:, pl.ds(place, 512)] = hidden
+            rest_ref[:, pl.ds(place, FFB)] = hidden
+
+    @pl.when(core == 0)
+    def _():
+        place_hidden(left_ref, send_ref)
+
+    @pl.when(core != 0)
+    def _():
+        place_hidden(send_ref, left_ref)
 
     @pl.when(step == FF_STEPS - 1)
     def _():

time: 462 us -> 461 us (level)
  no operation moved by 1% of the time
where the time goes in v1:
time: 461 us; the launch traced here: 457 us
  Pallas kernels  241 us (52%)
  waiting for transfers between devices  126 us (27%)
  starting transfers between devices  36 us (8%)
  other arithmetic  29.9 us (6%)
  between operations  16 us (3%)
  local copies, waits for them, and re-layouts  7.79 us (2%)
    ppermute x30, waiting for transfers between devices, swap(): return lax.ppermute(values, ('dp', 'shard'), pairs)  107 us
    pallas_call x6, Pallas kernels, adam_call(): pl.pallas_call(functools.partial(adam_kernel, route=route, joint=joint, p...  77.9 us
    pallas_call x1, Pallas kernels, backward(): pl.pallas_call(backward_kernel, grid_spec=pltpu.PrefetchScalarGridSpec(nu...  40.5 us
    pallas_call x1, Pallas kernels, unit(): pl.pallas_call(unit_kernel, grid_spec=pltpu.PrefetchScalarGridSpec(num_sc...  38.4 us
    ppermute x30, starting transfers between devices, swap(): return lax.ppermute(values, ('dp', 'shard'), pairs)  31.8 us
    pallas_call x2, Pallas kernels, grad_in(): pl.pallas_call(functools.partial(grad_in_kernel, route=route, lefts=len(l...  25.7 us
    pallas_call x1, Pallas kernels, forward(): pl.pallas_call(forward_kernel, grid_spec=pltpu.PrefetchScalarGridSpec(num...  23.7 us
    convert_element_type x18, other arithmetic, low(): return values.astype(jnp.bfloat16)  22 us
  transfers between devices with their start and end apart: 47, of which 15 were waited for; matrix products, arithmetic and copies ran while one was open for 8% of the time, Pallas kernels for 40%

profile of v1, /device:TPU:0, one launch (start us, length us, event | category | flops | bytes accessed | tf_op | source)
XLA Modules:
  0.0 456.9 jit_solution(2440888204273420199)
XLA Ops:
  7.2 6.5 %cast_out.1 = bf16[2560,1024]{1,0:T(8,128)(2,1)} custom-call(f32[2560,1024]{1,0:T(8,128)} %refs_2_.3), custom_call_target="tpu_custom_call" | custom-call | tf_op jit(solution)/shard_map/cast_out/pallas_call | solution.py:414
  17.6 5.7 %cast_qkv.1.own_ref = bf16[8,512,512]{2,1,0:T(8,128)(2,1)} custom-call(f32[512,10240]{1,0:T(8,128)} %refs_2_.5, f32[512,10240]{1,0:T(8,128)} %refs_2_.5, f32[512,10240]{1,0:T(8,128)} %refs_2_.5), custom_call_target="tpu_custom_call" | custom-call | tf_op jit(solution)/shard_map/cast_qkv/pallas_call | solution.py:392
  23.6 10.2 %cast_mix.1 = (bf16[3,256,2048]{2,1,0:T(8,128)(2,1)}, bf16[3,256,2048]{2,1,0:T(8,128)(2,1)}) custom-call(f32[512,10240]{1,0:T(8,128)} %refs_2_.5, f32[512,10240]{1,0:T(8,128)} %refs_2_.5), custom_call_target="tpu_custom_call" | custom-call | tf_op jit(solution)/shard_map/cast_mix/pallas_call | solution.py:439
  35.1 23.7 %forward.1 = (bf16[512,2048]{1,0:T(8,128)(2,1)}, bf16[8,512,512]{2,1,0:T(8,128)(2,1)}, f32[8,512,384]{2,1,0:T(8,128)}, f32[8,512,256]{2,1,0:T(8,128)}, bf16[512,...) custom-call(s32[6]{0:T(128)} %stack.26.meta_ref, bf16[512,1024]{1,0:T(8,128)(2,1)} %x_ref.2, ...), custom_call_target="tpu_custom_call" | custom-call | tf_op jit(solution)/shard_map/forward/pallas_call | solution.py:534
  61.2 38.4 %unit.1 = (bf16[512,1024]{1,0:T(8,128)(2,1)}, bf16[512,3072]{1,0:T(8,128)(2,1)}, bf16[512,3072]{1,0:T(8,128)(2,1)}, bf16[512,512]{1,0:T(8,128)(2,1)}, bf16[512,5...) custom-call(s32[6]{0:T(128)} %stack.26.meta_ref, ...), custom_call_target="tpu_custom_call" | custom-call | tf_op jit(solution)/shard_map/unit/pallas_call | solution.py:691
  100.7 5.7 %collective-permute-done.6.l_got.d_got = bf16[512,3584]{1,0:T(8,128)(2,1)} collective-permute-done((bf16[512,3584]{1,0:T(8,128)(2,1)}, bf16[512,3584]{1,0:T(8,128)(2,1)}, u32[]{:S(2)}, u32[]{:S(2)}) %collective-permute-start.6) | collective-permute-done | bytes 3670048 | tf_op jit(solution)/shard_map/ppermute | solution.py:1243
  106.4 12.7 %grad_out.1 = (bf16[640,1024]{1,0:T(8,128)(2,1)}, bf16[640,1024]{1,0:T(8,128)(2,1)}, bf16[640,1024]{1,0:T(8,128)(2,1)}, bf16[640,1024]{1,0:T(8,128)(2,1)}) custom-call(s32[6]{0:T(128)} %stack.26.meta_ref, bf16[512,2560]{1,0:T(8,128)(2,1)} %get-tuple-element.265.l_own, bf16[512,3584]{1,0:T(8,128)(2,1)} %collective-permute-done.6.l_got.d_got, ...), custom_call_target="tpu_custom_call" | custom-call | tf_op jit(solution)/shard_map/grad_out/pallas_call | solution.py:1017
  121.8 12.2 %grad_in.2 = (bf16[128,5120]{1,0:T(8,128)(2,1)}, bf16[128,5120]{1,0:T(8,128)(2,1)}, bf16[128,5120]{1,0:T(8,128)(2,1)}, bf16[128,5120]{1,0:T(8,128)(2,1)}) custom-call(s32[6]{0:T(128)} %stack.26.meta_ref, bf16[512,512]{1,0:T(8,128)(2,1)} %get-tuple-element.327.refs_0_.refs_2_, bf16[512,512]{1,0:T(8,128)(2,1)} %collective-permute-done.8.refs_1_.refs_3_, ...), custom_call_target="tpu_custom_call" | custom-call | tf_op jit(solution)/shard_map/grad_in/pallas_call | solution.py:969
  143.1 40.5 %backward.1 = (bf16[512,1024]{1,0:T(8,128)(2,1)}, bf16[512,1024]{1,0:T(8,128)(2,1)}, bf16[512,1024]{1,0:T(8,128)(2,1)}, bf16[512,1024]{1,0:T(8,128)(2,1)}, bf16[512,1024]{1,0:T(8,128)(2,1)}, /*index=5*/f32[8,1024]{1,0:T(8,128)}) custom-call(s32[6]{0:T(128)} %stack.26.meta_ref, f32[512,1024]{1,0:T(8,128)} %get-tuple-element.287.dmid_ref, ...), custom_call_target="tpu_custom_call" | custom-call | tf_op jit(solution)/shard_map/backward/pallas_call | solution.py:882
  196.5 7.0 %collective-permute-done.18 = bf16[128,5120]{1,0:T(8,128)(2,1)S(1)} collective-permute-done((bf16[128,5120]{1,0:T(8,128)(2,1)S(1)}, bf16[128,5120]{1,0:T(8,128)(2,1)S(1)}, u32[]{:S(2)}, u32[]{:S(2)}) %collective-permute-start.18) | collective-permute-done | bytes 1310752 | tf_op jit(solution)/shard_map/mix_halving_1/ppermute | solution.py:1073
  209.8 13.5 %grad_in.3 = (bf16[128,5120]{1,0:T(8,128)(2,1)}, bf16[128,5120]{1,0:T(8,128)(2,1)}, bf16[128,5120]{1,0:T(8,128)(2,1)}, bf16[128,5120]{1,0:T(8,128)(2,1)}) custom-call(s32[6]{0:T(128)} %stack.26.meta_ref, bf16[512,512]{1,0:T(8,128)(2,1)} %get-tuple-element.325.refs_0_, bf16[512,512]{1,0:T(8,128)(2,1)} %collective-permute-done.3.refs_1_, ...), custom_call_target="tpu_custom_call" | custom-call | tf_op jit(solution)/shard_map/grad_in/pallas_call | solution.py:969
  232.5 8.6 %collective-permute-done.24 = bf16[128,5120]{1,0:T(8,128)(2,1)S(1)} collective-permute-done((bf16[128,5120]{1,0:T(8,128)(2,1)}, bf16[128,5120]{1,0:T(8,128)(2,1)S(1)}, u32[]{:S(2)}, u32[]{:S(2)}) %collective-permute-start.24) | collective-permute-done | bytes 1310752 | tf_op jit(solution)/shard_map/qkv_halving_first_0/ppermute | solution.py:1073
  241.5 13.8 %collective-permute-done.23 = bf16[32,5120]{1,0:T(8,128)(2,1)S(1)} collective-permute-done((bf16[32,5120]{1,0:T(8,128)(2,1)S(1)}, bf16[32,5120]{1,0:T(8,128)(2,1)S(1)}, u32[]{:S(2)}, u32[]{:S(2)}) %collective-permute-start.23) | collective-permute-done | bytes 327712 | tf_op jit(solution)/shard_map/mix_halving_3/ppermute | solution.py:1073
  259.6 21.5 %collective-permute-done.25 = bf16[32,5120]{1,0:T(8,128)(2,1)S(1)} collective-permute-done((bf16[32,5120]{1,0:T(8,128)(2,1)S(1)}, bf16[32,5120]{1,0:T(8,128)(2,1)S(1)}, u32[]{:S(2)}, u32[]{:S(2)}) %collective-permute-start.25) | collective-permute-done | bytes 327712 | tf_op jit(solution)/shard_map/mix_doubling_3/ppermute | solution.py:1073
  291.9 8.2 %collective-permute-done.31 = bf16[64,5120]{1,0:T(8,128)(2,1)S(1)} collective-permute-done((bf16[64,5120]{1,0:T(8,128)(2,1)S(1)}, bf16[64,5120]{1,0:T(8,128)(2,1)S(1)}, u32[]{:S(2)}, u32[]{:S(2)}) %collective-permute-start.31) | collective-permute-done | bytes 655392 | tf_op jit(solution)/shard_map/mix_doubling_2/ppermute | solution.py:1073
  305.8 14.2 %collective-permute-done.34 = f32[8,1024]{1,0:T(8,128)S(1)} collective-permute-done((f32[8,1024]{1,0:T(8,128)S(1)}, f32[8,1024]{1,0:T(8,128)S(1)}, u32[]{:S(2)}, u32[]{:S(2)}) %collective-permute-start.34) | collective-permute-done | bytes 32800 | tf_op jit(solution)/shard_map/ppermute | solution.py:1073
  323.2 13.1 %adam.6 = (f32[512,10240]{1,0:T(8,128)}, f32[512,10240]{1,0:T(8,128)}, f32[512,10240]{1,0:T(8,128)}) custom-call(s32[6]{0:T(128)} %stack.26.meta_ref, bf16[128,5120]{1,0:T(8,128)(2,1)} %constant_dynamic-update-slice_fusion.4.refs_0_, bf16[128,5120]{1,0:T(8,128)(2,1)} %collective-permute-done.36.refs_1_, f32[512,10240]{1,0:T(8,128)} %refs_2_.5, ...), custom_call_target="tpu_custom_call" | custom-call | tf_op jit(solution)/shard_map/adam/pallas_call | solution.py:1214
  336.3 20.4 %collective-permute-done.35 = f32[8,1024]{1,0:T(8,128)} collective-permute-done((f32[8,1024]{1,0:T(8,128)}, f32[8,1024]{1,0:T(8,128)}, u32[]{:S(2)}, u32[]{:S(2)}) %collective-permute-start.35) | collective-permute-done | bytes 32800 | tf_op jit(solution)/shard_map/ppermute | solution.py:1073
  359.6 13.1 %adam.7 = (f32[2560,1024]{1,0:T(8,128)}, f32[2560,1024]{1,0:T(8,128)}, f32[2560,1024]{1,0:T(8,128)}) custom-call(s32[6]{0:T(128)} %stack.26.meta_ref, bf16[640,1024]{1,0:T(8,128)(2,1)} %constant_dynamic-update-slice_fusion.6.refs_0_, bf16[640,1024]{1,0:T(8,128)(2,1)} %collective-permute-done.33.refs_1_, f32[2560,1024]{1,0:T(8,128)} %refs_2_.3, ...), custom_call_target="tpu_custom_call" | custom-call | tf_op jit(solution)/shard_map/adam/pallas_call | solution.py:1214
  372.7 11.3 %all-reduce.2.cloned.1.call-done.refs_0_ = bf16[128,5120]{1,0:T(8,128)(2,1)} async-done(((bf16[128,5120]{1,0:T(8,128)(2,1)}), bf16[128,5120]{1,0:T(8,128)(2,1)}) %all-reduce.2.cloned.1.call-update) | async-done | bytes 1310736 | tf_op jit(solution)/shard_map/qkv_rest/psum | solution.py:1118
  387.0 12.9 %adam.8 = (f32[512,10240]{1,0:T(8,128)}, f32[512,10240]{1,0:T(8,128)}, f32[512,10240]{1,0:T(8,128)}) custom-call(s32[6]{0:T(128)} %stack.26.meta_ref, bf16[128,5120]{1,0:T(8,128)(2,1)} %collective-permute-done.41.refs_0_, bf16[128,5120]{1,0:T(8,128)(2,1)} %collective-permute-done.42.refs_1_, ...), custom_call_target="tpu_custom_call", output_to_operand_aliasing={{0}: (6, {}), {1}: (7, {}), {2}: (8, {})} | custom-call | tf_op jit(solution)/shard_map/adam/pallas_call | solution.py:1214
  399.9 12.9 %adam.9 = (f32[2560,1024]{1,0:T(8,128)}, f32[2560,1024]{1,0:T(8,128)}, f32[2560,1024]{1,0:T(8,128)}) custom-call(s32[6]{0:T(128)} %stack.26.meta_ref, bf16[640,1024]{1,0:T(8,128)(2,1)} %collective-permute-done.39.refs_0_, bf16[640,1024]{1,0:T(8,128)(2,1)} %collective-permute-done.40.refs_1_, ...), custom_call_target="tpu_custom_call", output_to_operand_aliasing={{0}: (6, {}), {1}: (7, {}), {2}: (8, {})} | custom-call | tf_op jit(solution)/shard_map/adam/pallas_call | solution.py:1214
  418.7 12.9 %adam.10 = (f32[512,10240]{1,0:T(8,128)}, f32[512,10240]{1,0:T(8,128)}, f32[512,10240]{1,0:T(8,128)}) custom-call(s32[6]{0:T(128)} %stack.26.meta_ref, bf16[128,5120]{1,0:T(8,128)(2,1)} %all-reduce.2.cloned.1.call-done.refs_0_, bf16[128,5120]{1,0:T(8,128)(2,1)} %collective-permute-done.38.refs_1_, ...), custom_call_target="tpu_custom_call", output_to_operand_aliasing={{0}: (6, {}), {1}: (7, {}), {2}: (8, {})} | custom-call | tf_op jit(solution)/shard_map/adam/pallas_call | solution.py:1214
  436.9 12.9 %adam.11 = (f32[512,10240]{1,0:T(8,128)}, f32[512,10240]{1,0:T(8,128)}, f32[512,10240]{1,0:T(8,128)}) custom-call(s32[6]{0:T(128)} %stack.26.meta_ref, bf16[128,5120]{1,0:T(8,128)(2,1)} %collective-permute-done.37.refs_0_, bf16[128,5120]{1,0:T(8,128)(2,1)} %collective-permute-done.43.refs_1_, ...), custom_call_target="tpu_custom_call", output_to_operand_aliasing={{0}: (6, {}), {1}: (7, {}), {2}: (8, {})} | custom-call | tf_op jit(solution)/shard_map/adam/pallas_call | solution.py:1214
  (163 shorter events, 88.6 us)
Async XLA Ops:
  7.2 54.0 %all-gather.2.cloned.1.call-start = ((), (), s32[]{:S(2)}) async-start(), calls=%async_computation | async-start | bytes 15728640 | tf_op jit(solution)/shard_map/all_gather | solution.py:1283
  13.8 370.3 %all-reduce.2.cloned.1.call-start = ((), (), s32[]{:S(2)}) async-start(), calls=%async_computation.1 | async-start | bytes 2621440 | tf_op jit(solution)/shard_map/qkv_rest/psum | solution.py:1118
  33.9 27.3 %collective-permute-start.4 = (bf16[3,256,2048]{2,1,0:T(8,128)(2,1)}, bf16[3,256,2048]{2,1,0:T(8,128)(2,1)}, u32[]{:S(2)}, u32[]{:S(2)}) collective-permute-start(bf16[3,256,2048]{2,1,0:T(8,128)(2,1)} %get-tuple-element.251.own_top_ref), channel_id=1, source_target_pairs={{0,1},{1,0},{2,3},{3,2},{4,5},{5,4},{6,7},{7,6},{8,9},{9,8},{10,11... | collective-permute-start | bytes 9437192 | tf_op jit(solution)/shard_map/ppermute | solution.py:1243
  34.0 27.1 %collective-permute-start.5 = (bf16[3,256,2048]{2,1,0:T(8,128)(2,1)}, bf16[3,256,2048]{2,1,0:T(8,128)(2,1)}, u32[]{:S(2)}, u32[]{:S(2)}) collective-permute-start(bf16[3,256,2048]{2,1,0:T(8,128)(2,1)} %get-tuple-element.252.own_end_ref), channel_id=1, source_target_pairs={{0,1},{1,0},{2,3},{3,2},{4,5},{5,4},{6,7},{7,6},{8,9},{9,8},{10,11... | collective-permute-start | bytes 9437192 | tf_op jit(solution)/shard_map/ppermute | solution.py:1243
  34.4 24.9 %collective-permute-start.2 = (bf16[512,1024]{1,0:T(8,128)(2,1)}, bf16[512,1024]{1,0:T(8,128)(2,1)}, u32[]{:S(2)}, u32[]{:S(2)}) collective-permute-start(bf16[512,1024]{1,0:T(8,128)(2,1)} %broadcast_select_fusion.e_ref.e_own), channel_id=1, source_target_pairs={{0,1},{1,0},{2,3},{3,2},{4,5},{5,4},{6,7},{7,6},{8,9},{9,8},{10,11... | collective-permute-start | bytes 3145736 | tf_op jit(solution)/shard_map/ppermute | solution.py:1243
  134.0 49.7 %collective-permute-start.17 = (bf16[128,5120]{1,0:T(8,128)(2,1)}, bf16[128,5120]{1,0:T(8,128)(2,1)}, u32[]{:S(2)}, u32[]{:S(2)}) collective-permute-start(bf16[128,5120]{1,0:T(8,128)(2,1)} %get-tuple-element.310), channel_id=1, source_target_pairs={{0,2},{1,5},{2,0},{3,7},{4,6},{5,1},{6,4},{7,3},{8,10},{9,13},{10,... | collective-permute-start | bytes 3932168 | tf_op jit(solution)/shard_map/mix_halving_first_0/ppermute | solution.py:1073
  134.0 53.5 %collective-permute-start.16 = (bf16[640,1024]{1,0:T(8,128)(2,1)}, bf16[640,1024]{1,0:T(8,128)(2,1)}, u32[]{:S(2)}, u32[]{:S(2)}) collective-permute-start(bf16[640,1024]{1,0:T(8,128)(2,1)} %get-tuple-element.308), channel_id=1, source_target_pairs={{0,2},{1,5},{2,0},{3,7},{4,6},{5,1},{6,4},{7,3},{8,10},{9,13},{10,... | collective-permute-start | bytes 3932168 | tf_op jit(solution)/shard_map/out_halving_0/ppermute | solution.py:1073
  136.0 53.3 %collective-permute-start.15 = (bf16[128,5120]{1,0:T(8,128)(2,1)}, bf16[128,5120]{1,0:T(8,128)(2,1)}, u32[]{:S(2)}, u32[]{:S(2)}) collective-permute-start(bf16[128,5120]{1,0:T(8,128)(2,1)} %get-tuple-element.307), channel_id=1, source_target_pairs={{0,2},{1,5},{2,0},{3,7},{4,6},{5,1},{6,4},{7,3},{8,10},{9,13},{10,... | collective-permute-start | bytes 3932168 | tf_op jit(solution)/shard_map/mix_halving_0/ppermute | solution.py:1073
  141.0 50.8 %collective-permute-start.19 = (bf16[640,1024]{1,0:T(8,128)(2,1)}, bf16[640,1024]{1,0:T(8,128)(2,1)}, u32[]{:S(2)}, u32[]{:S(2)}) collective-permute-start(bf16[640,1024]{1,0:T(8,128)(2,1)} %add_convert_fusion.6), channel_id=1, source_target_pairs={{0,8},{1,9},{2,10},{3,11},{4,12},{5,13},{6,14},{7,15},{8,0},{9,1},... | collective-permute-start | bytes 3932168 | tf_op jit(solution)/shard_map/out_halving_1/ppermute | solution.py:1073
  226.0 30.6 %collective-permute-start.26 = (bf16[160,1024]{1,0:T(8,128)(2,1)S(1)}, bf16[160,1024]{1,0:T(8,128)(2,1)S(1)}, u32[]{:S(2)}, u32[]{:S(2)}) collective-permute-start(bf16[160,1024]{1,0:T(8,128)(2,1)S(1)} %add_convert_fusion.16), channel_id=1, source_target_pairs={{0,16},{1,17},{2,18},{3,19},{4,20},{5,21},{6,22},{7,23},{8,24},{9,... | collective-permute-start | bytes 983048 | tf_op jit(solution)/shard_map/out_halving_3/ppermute | solution.py:1073
  231.1 24.2 %collective-permute-start.23 = (bf16[32,5120]{1,0:T(8,128)(2,1)S(1)}, bf16[32,5120]{1,0:T(8,128)(2,1)S(1)}, u32[]{:S(2)}, u32[]{:S(2)}) collective-permute-start(bf16[32,5120]{1,0:T(8,128)(2,1)S(1)} %add_convert_fusion.14), channel_id=1, source_target_pairs={{0,16},{1,17},{2,18},{3,19},{4,20},{5,21},{6,22},{7,23},{8,24},{9,... | collective-permute-start | bytes 983048 | tf_op jit(solution)/shard_map/mix_halving_3/ppermute | solution.py:1073
  255.4 25.7 %collective-permute-start.25 = (bf16[32,5120]{1,0:T(8,128)(2,1)S(1)}, bf16[32,5120]{1,0:T(8,128)(2,1)S(1)}, u32[]{:S(2)}, u32[]{:S(2)}) collective-permute-start(bf16[32,5120]{1,0:T(8,128)(2,1)S(1)} %add_convert_fusion.12), channel_id=1, source_target_pairs={{0,16},{1,17},{2,18},{3,19},{4,20},{5,21},{6,22},{7,23},{8,24},{9,... | collective-permute-start | bytes 983048 | tf_op jit(solution)/shard_map/mix_doubling_3/ppermute | solution.py:1073
  255.5 32.0 %collective-permute-start.28 = (f32[8,1024]{1,0:T(8,128)S(1)}, f32[8,1024]{1,0:T(8,128)S(1)}, u32[]{:S(2)}, u32[]{:S(2)}) collective-permute-start(f32[8,1024]{1,0:T(8,128)S(1)} %copy-done.14), channel_id=1, source_target_pairs={{0,1},{1,0},{2,3},{3,2},{4,5},{5,4},{6,7},{7,6},{8,9},{9,8},{10,11... | collective-permute-start | bytes 98312 | tf_op jit(solution)/shard_map/ppermute | solution.py:1243
  255.6 31.3 %collective-permute-start.20 = (bf16[128,5120]{1,0:T(8,128)(2,1)S(1)}, bf16[128,5120]{1,0:T(8,128)(2,1)S(1)}, u32[]{:S(2)}, u32[]{:S(2)}) collective-permute-start(bf16[128,5120]{1,0:T(8,128)(2,1)S(1)} %copy-done.16), channel_id=1, source_target_pairs={{0,2},{1,5},{2,0},{3,7},{4,6},{5,1},{6,4},{7,3},{8,10},{9,13},{10,... | collective-permute-start | bytes 3932168 | tf_op jit(solution)/shard_map/qkv_halving_0/ppermute | solution.py:1073
  256.1 32.0 %collective-permute-start.27 = (bf16[128,5120]{1,0:T(8,128)(2,1)S(1)}, bf16[128,5120]{1,0:T(8,128)(2,1)S(1)}, u32[]{:S(2)}, u32[]{:S(2)}) collective-permute-start(bf16[128,5120]{1,0:T(8,128)(2,1)S(1)} %add_convert_fusion.2), channel_id=1, source_target_pairs={{0,4},{1,3},{2,6},{3,1},{4,0},{5,7},{6,2},{7,5},{8,12},{9,11},{10,... | collective-permute-start | bytes 3932168 | tf_op jit(solution)/shard_map/qkv_halving_1/ppermute | solution.py:1073
  256.7 30.5 %collective-permute-start.29 = (bf16[160,1024]{1,0:T(8,128)(2,1)S(1)}, bf16[160,1024]{1,0:T(8,128)(2,1)S(1)}, u32[]{:S(2)}, u32[]{:S(2)}) collective-permute-start(bf16[160,1024]{1,0:T(8,128)(2,1)S(1)} %add_convert_fusion.11), channel_id=1, source_target_pairs={{0,16},{1,17},{2,18},{3,19},{4,20},{5,21},{6,22},{7,23},{8,24},{9,... | collective-permute-start | bytes 983048 | tf_op jit(solution)/shard_map/out_doubling_3/ppermute | solution.py:1073
  304.1 53.9 %collective-permute-start.33 = (bf16[640,1024]{1,0:T(8,128)(2,1)}, bf16[640,1024]{1,0:T(8,128)(2,1)}, u32[]{:S(2)}, u32[]{:S(2)}) collective-permute-start(bf16[640,1024]{1,0:T(8,128)(2,1)} %constant_dynamic-update-slice_fusion.6.refs_0_), channel_id=1, source_target_pairs={{0,8},{1,9},{2,10},{3,11},{4,12},{5,13},{6,14},{7,15},{8,0},{9,1},... | collective-permute-start | bytes 3932168 | tf_op jit(solution)/shard_map/out_doubling_1/ppermute | solution.py:1073
  320.7 36.0 %collective-permute-start.35 = (f32[8,1024]{1,0:T(8,128)}, f32[8,1024]{1,0:T(8,128)}, u32[]{:S(2)}, u32[]{:S(2)}) collective-permute-start(f32[8,1024]{1,0:T(8,128)} %add.162), channel_id=1, source_target_pairs={{0,8},{1,9},{2,10},{3,11},{4,12},{5,13},{6,14},{7,15},{8,0},{9,1},... | collective-permute-start | bytes 98312 | tf_op jit(solution)/shard_map/ppermute | solution.py:1073
  320.7 64.8 %collective-permute-start.41 = (bf16[128,5120]{1,0:T(8,128)(2,1)}, bf16[128,5120]{1,0:T(8,128)(2,1)}, u32[]{:S(2)}, u32[]{:S(2)}) collective-permute-start(bf16[128,5120]{1,0:T(8,128)(2,1)} %constant_dynamic-update-slice_fusion.4.refs_0_), channel_id=1, source_target_pairs={{0,2},{1,5},{2,0},{3,7},{4,6},{5,1},{6,4},{7,3},{8,10},{9,13},{10,... | collective-permute-start | bytes 3932168 | tf_op jit(solution)/shard_map/mix_doubling_0/ppermute | solution.py:1073
  321.2 78.7 %collective-permute-start.39 = (bf16[640,1024]{1,0:T(8,128)(2,1)}, bf16[640,1024]{1,0:T(8,128)(2,1)}, u32[]{:S(2)}, u32[]{:S(2)}) collective-permute-start(bf16[640,1024]{1,0:T(8,128)(2,1)} %constant_dynamic-update-slice_fusion.6.refs_0_), channel_id=1, source_target_pairs={{0,2},{1,5},{2,0},{3,7},{4,6},{5,1},{6,4},{7,3},{8,10},{9,13},{10,... | collective-permute-start | bytes 3932168 | tf_op jit(solution)/shard_map/out_doubling_0/ppermute | solution.py:1073
  322.7 64.3 %collective-permute-start.42 = (bf16[128,5120]{1,0:T(8,128)(2,1)}, bf16[128,5120]{1,0:T(8,128)(2,1)}, u32[]{:S(2)}, u32[]{:S(2)}) collective-permute-start(bf16[128,5120]{1,0:T(8,128)(2,1)} %collective-permute-done.36.refs_1_), channel_id=1, source_target_pairs={{0,2},{1,5},{2,0},{3,7},{4,6},{5,1},{6,4},{7,3},{8,10},{9,13},{10,... | collective-permute-start | bytes 3932168 | tf_op jit(solution)/shard_map/mix_doubling_last_0/ppermute | solution.py:1073
  358.1 41.8 %collective-permute-start.40 = (bf16[640,1024]{1,0:T(8,128)(2,1)}, bf16[640,1024]{1,0:T(8,128)(2,1)}, u32[]{:S(2)}, u32[]{:S(2)}) collective-permute-start(bf16[640,1024]{1,0:T(8,128)(2,1)} %collective-permute-done.33.refs_1_), channel_id=1, source_target_pairs={{0,2},{1,5},{2,0},{3,7},{4,6},{5,1},{6,4},{7,3},{8,10},{9,13},{10,... | collective-permute-start | bytes 3932168 | tf_op jit(solution)/shard_map/out_doubling_last_0/ppermute | solution.py:1073
  384.0 32.0 %collective-permute-start.38 = (bf16[128,5120]{1,0:T(8,128)(2,1)}, bf16[128,5120]{1,0:T(8,128)(2,1)}, u32[]{:S(2)}, u32[]{:S(2)}) collective-permute-start(bf16[128,5120]{1,0:T(8,128)(2,1)} %all-reduce.2.cloned.1.call-done.refs_0_), channel_id=1, source_target_pairs={{0,4},{1,3},{2,6},{3,1},{4,0},{5,7},{6,2},{7,5},{8,12},{9,11},{10,... | collective-permute-start | bytes 3932168 | tf_op jit(solution)/shard_map/qkv_doubling_1/ppermute | solution.py:1073
  385.5 51.4 %collective-permute-start.37 = (bf16[128,5120]{1,0:T(8,128)(2,1)}, bf16[128,5120]{1,0:T(8,128)(2,1)}, u32[]{:S(2)}, u32[]{:S(2)}) collective-permute-start(bf16[128,5120]{1,0:T(8,128)(2,1)} %all-reduce.2.cloned.1.call-done.refs_0_), channel_id=1, source_target_pairs={{0,2},{1,5},{2,0},{3,7},{4,6},{5,1},{6,4},{7,3},{8,10},{9,13},{10,... | collective-permute-start | bytes 3932168 | tf_op jit(solution)/shard_map/qkv_doubling_0/ppermute | solution.py:1073
  (40 other events, 478.8 us)
Sparse Core Ops, SparseCore 0:
  13.9 29.8 all-gather.1
  304.3 79.7 all-reduce.1
